TPU v7x, 256 devices: a whole 4x4x8 slice. The times are simulated.
256 devices in a mesh: dp: 32 (over z, y), expert: 8 (over x, core).
Axes of the slice: x: 4, y: 4, z: 8, core: 2. Of those that a mesh axis runs over, the one named last changes fastest.
Arguments:
- grad_out: bfloat16 [131072, 4096], P(('dp', 'expert')), may hold values from -6 to 6
- expert_ids: int32 [131072, 8], P(('dp', 'expert')), may hold values from 0 to 127, as said below
- route_weights: bfloat16 [131072, 8], P(('dp', 'expert')), may hold values from 0.049804688 to 0.5
- saved_preact: bfloat16 [8, 32, 8, 64, 3072], P('expert', 'dp'), may hold values from -6 to 6
- down_weight: bfloat16 [8, 1536, 4096], P('expert', 'dp'), may hold values from -0.15625 to 0.15625
Outputs:
- route_grad: float32 [131072, 8], P(('dp', 'expert'))
- preact_grad: bfloat16 [8, 32, 8, 64, 3072], P('expert', 'dp')
- down_grad: float32 [8, 1536, 4096], P('expert', 'dp')
Inputs may be any that keep to these rules, and one draw needn't show every extreme that they name: `expert_ids`: each token's 8 ids are distinct. At most 64 tokens of one device name any one expert below 8; in every data index, some expert below 8 is named by exactly 64 tokens of each of its 8 devices.
All inputs are finite; a program needn't handle non-finite values.
Results may differ from a plain program's by a relative error of at most 0.024.
Values may be sent and summed in bfloat16 or wider, within the bound.
No kernel may reach another device: no remote copies, remote signals or barrier semaphores. Data moves between devices by JAX's collectives and lax.ppermute only.
A program may use at most 128 MiB of HBM per device.

v0:
```python
import jax
import jax.numpy as jnp
from jax import lax
from jax.sharding import PartitionSpec as P


def slot_tables(block_ids, block_weights, flight, capacity):
    labels = jnp.arange(flight, dtype=jnp.int32)
    hits = block_ids[:, :, None] == labels[None, None, :]
    member = jnp.any(hits, axis=1).astype(jnp.int32)
    chosen = jnp.sum(
        jnp.where(hits, block_weights.astype(jnp.float32)[:, :, None], jnp.float32(0.0)), axis=1
    )
    rank = jnp.cumsum(member, axis=0) - member
    where_to = jnp.where(member == 1, labels[None, :] * capacity + rank, flight * capacity).reshape(
        -1
    )
    token_of = jnp.broadcast_to(
        jnp.arange(block_ids.shape[0], dtype=jnp.int32)[:, None], member.shape
    ).reshape(-1)
    slot_token = (
        jnp.zeros((flight * capacity + 1,), jnp.int32)
        .at[where_to]
        .set(token_of)[: flight * capacity]
    )
    slot_weight = (
        jnp.zeros((flight * capacity + 1,), jnp.float32)
        .at[where_to]
        .set(chosen.reshape(-1))[: flight * capacity]
    )
    return (slot_token, slot_weight.astype(jnp.bfloat16), rank)


def per_device(grad_out, expert_ids, route_weights, saved_preact, down_weight):
    flight = lax.axis_size("expert")
    capacity = saved_preact.shape[3]
    hidden_units = saved_preact.shape[4] // 2
    width = grad_out.shape[1]
    slot_token, slot_weight, rank = slot_tables(expert_ids, route_weights, flight, capacity)
    picked = grad_out[slot_token]
    picked = jnp.where((slot_weight > 0)[:, None], picked, jnp.zeros_like(picked))
    send_rows = picked.reshape(flight, capacity, width)
    send_weights = slot_weight.reshape(flight, capacity)
    total_rows = flight * capacity
    stored = down_weight[0]
    preact = saved_preact[0, 0].reshape(total_rows, 2 * hidden_units)
    gate = preact[:, :hidden_units].astype(jnp.float32)
    upper = preact[:, hidden_units:].astype(jnp.float32)
    sig = jax.nn.sigmoid(gate)
    hidden = (gate * sig * upper).astype(jnp.bfloat16)
    got_rows, got_weights = (
        lax.all_to_all(send_rows, "expert", split_axis=0, concat_axis=0, tiled=True),
        lax.all_to_all(send_weights, "expert", split_axis=0, concat_axis=0, tiled=True),
    )
    gathered_rows = got_rows.reshape(total_rows, width)
    scale = got_weights.reshape(total_rows).astype(jnp.float32)[:, None]
    scaled = (scale * hidden.astype(jnp.float32)).astype(jnp.bfloat16)
    act_grad = lax.dot_general(
        gathered_rows,
        lax.all_gather(stored, "dp", axis=0, tiled=True),
        (((1,), (1,)), ((), ())),
        preferred_element_type=jnp.float32,
    )
    own_rows = lax.psum_scatter(
        lax.dot_general(
            scaled, gathered_rows, (((0,), (0,)), ((), ())), preferred_element_type=jnp.float32
        ).astype(jnp.bfloat16),
        "dp",
        scatter_dimension=0,
        tiled=True,
    ).astype(jnp.float32)
    slot_route = jnp.sum(act_grad * hidden.astype(jnp.float32), axis=1)
    dh_val = scale * act_grad
    gate_grad = dh_val * upper * sig * (1.0 + gate * (1.0 - sig))
    upper_grad = dh_val * gate * sig
    preact_grad = jnp.concatenate([gate_grad, upper_grad], axis=1).astype(jnp.bfloat16)
    preact_grad = preact_grad.reshape(1, 1, flight, capacity, 2 * hidden_units)
    returned = lax.all_to_all(
        slot_route.reshape(flight, capacity), "expert", split_axis=0, concat_axis=0, tiled=True
    )
    clipped = jnp.clip(expert_ids, 0, flight - 1)
    rank_k = jnp.take_along_axis(rank, clipped, axis=1)
    index = jnp.where(expert_ids < flight, expert_ids * capacity + rank_k, flight * capacity)
    padded = jnp.concatenate([returned.reshape(-1), jnp.zeros((1,), jnp.float32)])
    route_grad = padded[index]
    return (route_grad, preact_grad, own_rows[None])


def solution(mesh):
    return jax.shard_map(
        per_device,
        mesh=mesh,
        in_specs=(
            P(("dp", "expert"), None),
            P(("dp", "expert"), None),
            P(("dp", "expert"), None),
            P("expert", "dp", None, None, None),
            P("expert", "dp", None),
        ),
        out_specs=(
            P(("dp", "expert"), None),
            P("expert", "dp", None, None, None),
            P("expert", "dp", None),
        ),
        check_vma=False,
    )
```

profile of v0, /device:TPU:1, one launch (start us, length us, event | category | flops | bytes accessed | tf_op | source)
XLA Modules:
  0.0 378.0 jit_solution(18015488166472694792)
XLA Ops:
  7.2 0.7 all-gather.3.cloned.1.call-update
  7.9 0.7 fusion.16
  8.7 1.1 reduce-window.6
  10.5 0.7 convert_element_type.66
  11.2 0.7 select_reduce_fusion
  12.2 15.5 %scatter_custom_fusion = f32[513]{0:T(1024)S(1)} fusion(s32[4096]{0:T(1024)S(1)} %bitcast.32, f32[4096]{0:T(1024)S(1)} %reshape.186, f32[]{:T(128)} %constant.13.clone.1), kind=kCustom, calls=%fused_computation.52 | custom fusion | bytes 2056 | tf_op jit(solution)/shard_map/scatter | solution.py:29
  27.7 0.7 convert_element_type.78
  28.4 6.5 %all-to-all-start.2 = ((bf16[8,1,64]{2,1,0:T(2,128)(2,1)}), bf16[8,1,64]{2,1,0:T(2,128)(2,1)S(1)}, u32[]{:S(2)}, u32[]{:S(2)}) async-start(bf16[8,1,64]{2,1,0:T(2,128)(2,1)} %convert_element_type.78), calls=%async_computation.2 | async-start | bytes 8192 | tf_op jit(solution)/shard_map/all_to_all | solution.py:53
  35.1 15.5 %scatter_custom_fusion.1 = s32[513]{0:T(1024)S(1)} fusion(s32[4096]{0:T(1024)S(1)} %bitcast.33, s32[4096]{0:T(1024)S(1)} %reshape.194, s32[]{:T(128)} %constant.17.clone.1), kind=kCustom, calls=%fused_computation.49 | custom fusion | bytes 2056 | tf_op jit(solution)/shard_map/scatter | solution.py:24
  50.7 11.3 %gather_fusion = bf16[512,4096]{1,0:T(8,128)(2,1)} fusion(bf16[512,4096]{1,0:T(8,128)(2,1)} %param.5, s32[1024]{0:T(1024)S(1)} %pad_clamp_fusion), kind=kCustom, calls=%fused_computation | custom fusion | bytes 8390656 | tf_op jit(solution)/shard_map/gather | solution.py:40
  62.0 4.5 %broadcast_select_fusion = bf16[8,64,4096]{2,1,0:T(8,128)(2,1)} fusion(bf16[8,64,4096]{2,1,0:T(8,128)(2,1)} %bitcast.29, pred[8,64]{1,0:T(8,128)(4,1)S(1)} %gt.12), kind=kLoop, calls=%fused_computation.12 | loop fusion | flops 2097152 | bytes 8389120 | tf_op jit(solution)/shard_map/jit(_where)/select_n | solution.py:41
  66.5 4.8 %all-to-all-start = ((bf16[8,64,4096]{2,1,0:T(8,128)(2,1)}), bf16[8,64,4096]{2,1,0:T(8,128)(2,1)}, u32[]{:S(2)}, u32[]{:S(2)}) async-start(bf16[8,64,4096]{2,1,0:T(8,128)(2,1)} %broadcast_select_fusion), calls=%async_computation | async-start | bytes 8388608 | tf_op jit(solution)/shard_map/all_to_all | solution.py:52
  71.4 48.8 %all-to-all-done = bf16[8,64,4096]{2,1,0:T(8,128)(2,1)} async-done(((bf16[8,64,4096]{2,1,0:T(8,128)(2,1)}), bf16[8,64,4096]{2,1,0:T(8,128)(2,1)}, u32[]{:S(2)}, u32[]{:S(2)}) %all-to-all-start) | async-done | bytes 4194336 | tf_op jit(solution)/shard_map/all_to_all | solution.py:52
  120.2 12.8 %convolution_convert_fusion = bf16[1536,4096]{1,0:T(8,128)(2,1)} fusion(bf16[512,4096]{1,0:T(8,128)(2,1)} %bitcast.6, f32[512]{0:T(512)S(1)} %reshape.158, bf16[512,3072]{1,0:T(8,128)(2,1)} %bitcast.34), kind=kOutput, calls=%fused_computation.5 | convolution fusion | flops 6457393152 | bytes 19924992 | tf_op jit(solution)/shard_map/dot_general | solution.py:65
  133.0 0.7 copy-done
  134.0 24.5 %gather_fusion.2 = s32[4096]{0:T(1024)S(1)} fusion(s32[512,8]{0,1:T(8,128)S(1)} %get-tuple-element.15, s32[4096]{0:T(1024)S(1)} %reshape.176), kind=kCustom, calls=%fused_computation.2 | custom fusion | bytes 65536 | tf_op jit(solution)/shard_map/jit(take_along_axis)/gather | solution.py:82
  159.2 13.5 %fusion.5 = (bf16[512,1536]{1,0:T(8,128)(2,1)S(1)}, bf16[512,1536]{1,0:T(8,128)(2,1)S(1)}, f32[512]{0:T(512)S(1)}) fusion(f32[512]{0:T(512)S(1)} %reshape.158, bf16[512,3072]{1,0:T(8,128)(2,1)} %bitcast.35, bf16[512,4096]{1,0:T(8,128)(2,1)} %bitcast.6, bf16[1,1536,4096]{2,1,0:T(8,128)(2,1)} %all-gather.3.cloned.1.call-done), kind=kOutput, calls=%fused_computation.20 | convolution fusion | flops 6459751936 | bytes 23072768 | tf_op jit(solution)/shard_map/dot_general | solution.py:58
  173.3 4.0 %all-to-all-start.1 = ((f32[8,1,64]{2,1,0:T(1,128)}), f32[8,1,64]{2,1,0:T(1,128)S(1)}, u32[]{:S(2)}, u32[]{:S(2)}) async-start(f32[8,1,64]{2,1,0:T(1,128)} %all_to_all.14), calls=%async_computation.1 | async-start | bytes 8192 | tf_op jit(solution)/shard_map/all_to_all | solution.py:78
  177.4 2.1 pad_maximum_fusion
  179.4 2.4 all-to-all-done.1
  183.1 16.7 %gather_fusion.1 = f32[4096]{0:T(1024)S(1)} fusion(f32[513]{0:T(1024)S(1)} %pad_maximum_fusion.1, s32[4096]{0:T(1024)S(1)} %broadcast_clamp_fusion), kind=kCustom, calls=%fused_computation.1 | custom fusion | bytes 49152 | tf_op jit(solution)/shard_map/gather | solution.py:85
  200.0 0.7 copy.31
  200.7 168.6 %reduce-scatter.2.cloned.1.call-done = bf16[48,4096]{1,0:T(8,128)(2,1)} async-done(((bf16[1536,4096]{1,0:T(8,128)(2,1)}), bf16[48,4096]{1,0:T(8,128)(2,1)}) %reduce-scatter.2.cloned.1.call-update) | async-done | bytes 393232 | tf_op jit(solution)/shard_map/reduce_scatter | solution.py:64
  369.3 1.9 bitcast_convert_fusion
  (40 shorter events, 4.3 us)
Async XLA Ops:
  7.2 152.0 %all-gather.3.cloned.1.call-start = ((), (), s32[]{:S(2)}) async-start(), calls=%async_computation.5 | async-start | bytes 12976128 | tf_op jit(solution)/shard_map/all_gather | solution.py:60
  28.4 38.1 %all-to-all-start.2 = ((bf16[8,1,64]{2,1,0:T(2,128)(2,1)}), bf16[8,1,64]{2,1,0:T(2,128)(2,1)S(1)}, u32[]{:S(2)}, u32[]{:S(2)}) async-start(bf16[8,1,64]{2,1,0:T(2,128)(2,1)} %convert_element_type.78), calls=%async_computation.2 | async-start | bytes 8192 | tf_op jit(solution)/shard_map/all_to_all | solution.py:53
  66.5 53.7 %all-to-all-start = ((bf16[8,64,4096]{2,1,0:T(8,128)(2,1)}), bf16[8,64,4096]{2,1,0:T(8,128)(2,1)}, u32[]{:S(2)}, u32[]{:S(2)}) async-start(bf16[8,64,4096]{2,1,0:T(8,128)(2,1)} %broadcast_select_fusion), calls=%async_computation | async-start | bytes 8388608 | tf_op jit(solution)/shard_map/all_to_all | solution.py:52
  71.3 298.0 %reduce-scatter.2.cloned.1.call-start = ((), (), s32[]{:S(2)}) async-start(), calls=%async_computation.4 | async-start | bytes 12976128 | tf_op jit(solution)/shard_map/reduce_scatter | solution.py:64
  133.0 0.7 copy-start
  173.3 8.6 %all-to-all-start.1 = ((f32[8,1,64]{2,1,0:T(1,128)}), f32[8,1,64]{2,1,0:T(1,128)S(1)}, u32[]{:S(2)}, u32[]{:S(2)}) async-start(f32[8,1,64]{2,1,0:T(1,128)} %all_to_all.14), calls=%async_computation.1 | async-start | bytes 8192 | tf_op jit(solution)/shard_map/all_to_all | solution.py:78
Sparse Core Ops, SparseCore 0:
  10.6 123.1 all-gather.2
  137.9 231.3 reduce-scatter.1
where the time goes:
time: 382 us; the launch traced here: 378 us
  waiting for transfers between devices  221 us (58%)
  local copies, waits for them, and re-layouts  88.9 us (23%)
  matrix products  26.3 us (7%)
  starting transfers between devices  15.4 us (4%)
  between operations  14.2 us (4%)
  other arithmetic  12.7 us (3%)
    reduce_scatter x1, waiting for transfers between devices, per_device(): lax.psum_scatter(lax.dot_general(scaled, gathered_rows, (((0,), (0,)), ((...  169 us
    all_to_all x1, waiting for transfers between devices, per_device(): lax.all_to_all(send_rows, 'expert', split_axis=0, concat_axis=0, tiled=True)  48.8 us
    gather x5, local copies, waits for them, and re-layouts, per_device(): rank_k = jnp.take_along_axis(rank, clipped, axis=1)  25 us
    gather x2, local copies, waits for them, and re-layouts, per_device(): route_grad = padded[index]  16.8 us
    scatter x1, local copies, waits for them, and re-layouts, slot_tables(): slot_weight = jnp.zeros((flight * capacity + 1,), jnp.float32).at[where_t...  15.5 us
    scatter x1, local copies, waits for them, and re-layouts, slot_tables(): slot_token = jnp.zeros((flight * capacity + 1,), jnp.int32).at[where_to]....  15.5 us
    dot_general x1, matrix products, per_device(): lax.dot_general(gathered_rows, lax.all_gather(stored, 'dp', axis=0, tiled...  13.5 us
    dot_general x1, matrix products, per_device(): lax.dot_general(scaled, gathered_rows, (((0,), (0,)), ((), ())), preferre...  12.8 us
  transfers between devices with their start and end apart: 5, of which 3 were waited for; matrix products, arithmetic and copies ran while one was open for 33% of the time, Pallas kernels for 0%

commit v1 on v0

v1 whole, which is shorter than its diff:
```python
import functools

import jax
import jax.numpy as jnp
from jax import lax
from jax.experimental import pallas as pl
from jax.experimental.pallas import tpu as pltpu
from jax.sharding import PartitionSpec as P

F32 = jnp.float32
BF16 = jnp.bfloat16
LANES = 128
TILE = 512
NY = 4
NZ = 8
VMEM_LIMIT = 40 * 1024 * 1024


def params(grid_rank):
    return pltpu.CompilerParams(
        dimension_semantics=("arbitrary",) * grid_rank, vmem_limit_bytes=VMEM_LIMIT
    )


def cost(flops, moved):
    return pl.CostEstimate(flops=flops, bytes_accessed=moved, transcendentals=0)


def whole(shape):
    return pl.BlockSpec(shape, lambda *_: (0,) * len(shape))


def table_kernel(flight, capacity, width, ids_ref, w_ref, g_ref, rows_ref, onehot_ref, rank_ref):
    ids = ids_ref[...]
    weights = w_ref[...].astype(F32)
    tokens = ids.shape[1]
    member, chosen = [], []
    for e in range(flight):
        hit = ids == e
        member.append(jnp.max(jnp.where(hit, 1.0, 0.0), axis=0, keepdims=True))
        chosen.append(jnp.sum(jnp.where(hit, weights, 0.0), axis=0, keepdims=True))
    member = jnp.concatenate(member, axis=0)
    before = lax.broadcasted_iota(jnp.int32, (tokens, tokens), 0) < lax.broadcasted_iota(
        jnp.int32, (tokens, tokens), 1
    )
    rank = jnp.dot(
        member.astype(BF16), jnp.where(before, 1.0, 0.0).astype(BF16), preferred_element_type=F32
    )
    rank = jnp.where(member > 0.0, rank, -1.0)
    rank_ref[...] = rank
    slot = lax.broadcasted_iota(jnp.int32, (capacity, tokens), 0).astype(F32)
    for e in range(flight):
        here = rank[e : e + 1, :] == slot
        onehot_ref[e * capacity : (e + 1) * capacity, :] = jnp.where(here, 1.0, 0.0).astype(BF16)
        column = jnp.sum(jnp.where(here, chosen[e], 0.0), axis=1, keepdims=True)
        rows_ref[e * capacity : (e + 1) * capacity, width:] = jnp.broadcast_to(
            column, (capacity, LANES)
        ).astype(BF16)
    onehot = onehot_ref[...]
    for at in range(0, width, TILE):
        rows_ref[:, at : at + TILE] = jnp.dot(
            onehot, g_ref[:, at : at + TILE], preferred_element_type=F32
        ).astype(BF16)


def tables(ids_t, weights_t, grad_out, flight, capacity, width):
    tokens = grad_out.shape[0]
    slots = flight * capacity
    return pl.pallas_call(
        functools.partial(table_kernel, flight, capacity, width),
        grid=(1,),
        in_specs=[
            whole(ids_t.shape),
            whole(weights_t.shape),
            pl.BlockSpec((tokens, width), lambda i: (0, 0)),
        ],
        out_specs=[whole((slots, width + LANES)), whole((slots, tokens)), whole((flight, tokens))],
        out_shape=[
            jax.ShapeDtypeStruct((slots, width + LANES), BF16),
            jax.ShapeDtypeStruct((slots, tokens), BF16),
            jax.ShapeDtypeStruct((flight, tokens), F32),
        ],
        compiler_params=params(1),
        cost_estimate=cost(2 * slots * tokens * width, 4 * tokens * width + 2 * slots * tokens),
        name="tables",
    )(ids_t, weights_t, grad_out)


def pick_kernel(onehot_ref, g_ref, rows_ref):
    rows_ref[...] = jnp.dot(onehot_ref[...], g_ref[...], preferred_element_type=F32).astype(BF16)


def pick(onehot, grad_out, start, width):
    slots, tokens = onehot.shape
    first = start // TILE
    return pl.pallas_call(
        pick_kernel,
        grid=(width // TILE,),
        in_specs=[
            whole(onehot.shape),
            pl.BlockSpec((tokens, TILE), lambda i: (0, first + i)),
        ],
        out_specs=pl.BlockSpec((slots, TILE), lambda i: (0, i)),
        out_shape=jax.ShapeDtypeStruct((slots, width), BF16),
        compiler_params=params(1),
        cost_estimate=cost(2 * slots * tokens * width, 4 * tokens * width + 2 * slots * tokens),
        name="pick",
    )(onehot, grad_out)


def hidden_kernel(gate_ref, up_ref, out_ref):
    gate = gate_ref[...].astype(F32)
    out_ref[...] = (gate * jax.nn.sigmoid(gate) * up_ref[...].astype(F32)).T.astype(BF16)


def hidden_transposed(preact):
    rows, both = preact.shape
    units = both // 2
    block = 256
    count = units // block
    return pl.pallas_call(
        hidden_kernel,
        grid=(count,),
        in_specs=[
            pl.BlockSpec((rows, block), lambda i: (0, i)),
            pl.BlockSpec((rows, block), lambda i: (0, count + i)),
        ],
        out_specs=pl.BlockSpec((block, rows), lambda i: (i, 0)),
        out_shape=jax.ShapeDtypeStruct((units, rows), BF16),
        compiler_params=params(1),
        cost_estimate=cost(10 * rows * units, 6 * rows * units),
        name="hidden",
    )(preact, preact)


def scale_kernel(w_ref, out_ref):
    out_ref[...] = w_ref[...].astype(F32).T[:8, :]


def scale_row(got, width):
    rows = got.shape[0]
    return pl.pallas_call(
        scale_kernel,
        grid=(1,),
        in_specs=[pl.BlockSpec((rows, LANES), lambda i: (0, width // LANES))],
        out_specs=whole((8, rows)),
        out_shape=jax.ShapeDtypeStruct((8, rows), F32),
        compiler_params=params(1),
        cost_estimate=cost(0, 2 * rows * LANES),
        name="scale",
    )(got)


def product(hidden_ref, scale_ref, rows_ref):
    hidden = hidden_ref[...]
    hidden = hidden.reshape(-1, hidden.shape[-1]).astype(F32)
    scaled = (hidden * scale_ref[0:1, :]).astype(BF16)
    return jnp.dot(scaled, rows_ref[...], preferred_element_type=F32)


def first_kernel(at_ref, hid_ref, scale_ref, rows_ref, down_ref, up_ref):
    value = product(hid_ref, scale_ref, rows_ref).astype(BF16)
    half = value.shape[0] // 2
    down_ref[...] = value[:half]
    up_ref[...] = value[half:]


def middle_kernel(at_ref, hid_d, hid_u, scale_ref, rows_ref, got_d, got_u, down_ref, up_ref):
    down = product(hid_d, scale_ref, rows_ref)
    up = product(hid_u, scale_ref, rows_ref)
    size, part = down.shape[0], got_d.shape[0]
    if part == size:
        down_ref[...] = (down + got_d[...].astype(F32)).astype(BF16)
        up_ref[...] = (up + got_u[...].astype(F32)).astype(BF16)
    else:
        down_ref[:part] = (down[:part] + got_d[...].astype(F32)).astype(BF16)
        down_ref[part:] = down[part:].astype(BF16)
        up_ref[:part] = up[:part].astype(BF16)
        up_ref[part:] = (up[part:] + got_u[...].astype(F32)).astype(BF16)


def last_kernel(at_ref, hid_ref, scale_ref, rows_ref, got_d, got_u, out_ref):
    own = product(hid_ref, scale_ref, rows_ref)
    out_ref[...] = (own + got_d[...].astype(F32) + got_u[...].astype(F32)).astype(BF16)


def neighbours(axis, step):
    pairs = []
    for z in range(NZ):
        for y in range(NY):
            to = ((z + step) % NZ, y) if axis == "z" else (z, (y + step) % NY)
            pairs.append((z * NY + y, to[0] * NY + to[1]))
    return pairs


def ring(axis, place, hidden, scale, rows, width):
    units, depth = hidden.shape
    shard = units // (NZ * NY)
    if axis == "z":
        size, slot = NZ, 0
        hidden = hidden.reshape(NZ, NY * shard, depth)
        hid_shape = (1, NY * shard, depth)
    else:
        size, slot = NY, 1
        hidden = hidden.reshape(NZ, NY, shard, depth)
        hid_shape = (NZ, 1, shard, depth)
    block = units // size
    half = size // 2
    tiles = width // TILE

    def hid(offset):
        def target(at):
            return (at[slot] + (offset + size)) & (size - 1)

        if axis == "z":
            return pl.BlockSpec(hid_shape, lambda i, at: (target(at), 0, 0))
        return pl.BlockSpec(hid_shape, lambda i, at: (0, target(at), 0, 0))

    def tile(n):
        return pl.BlockSpec((n, TILE), lambda i, at: (0, i))

    common = [pl.BlockSpec(scale.shape, lambda i, at: (0, 0)), tile(depth)]

    def call(kernel, offsets, arrived, outs, name):
        return pl.pallas_call(
            kernel,
            grid_spec=pltpu.PrefetchScalarGridSpec(
                num_scalar_prefetch=1,
                grid=(tiles,),
                in_specs=[hid(o) for o in offsets]
                + common
                + [tile(a.shape[0]) for a in arrived],
                out_specs=[tile(n) for n in outs],
            ),
            out_shape=[jax.ShapeDtypeStruct((n, width), BF16) for n in outs],
            compiler_params=params(1),
            cost_estimate=cost(
                2 * block * depth * width * len(offsets),
                2 * width * (depth + sum(outs) + sum(a.shape[0] for a in arrived)),
            ),
            name=name,
        )(place, *[hidden] * len(offsets), scale, rows, *arrived)

    def send(down, up):
        return [
            lax.ppermute(down, "dp", neighbours(axis, -1)),
            lax.ppermute(up, "dp", neighbours(axis, 1)),
        ]

    arrived = send(*call(first_kernel, [half], [], [block // 2] * 2, "first_" + axis))
    for s in range(1, half):
        arrived = send(
            *call(middle_kernel, [s - half, half - s], arrived, [block] * 2, "middle_" + axis)
        )
    return call(last_kernel, [0], arrived, [block], "last_" + axis)[0]


def exchange(part, axis):
    if axis == "z":
        size, groups = NZ, [[z * NY + y for z in range(NZ)] for y in range(NY)]
    else:
        size, groups = NY, [[z * NY + y for y in range(NY)] for z in range(NZ)]
    part = part.reshape(size, part.shape[0] // size, part.shape[1])
    return lax.all_to_all(
        part, "dp", split_axis=0, concat_axis=0, tiled=True, axis_index_groups=groups
    )


def sum_kernel(count_a, a_ref, b_ref, out_ref):
    step = pl.program_id(0)

    @pl.when(step < count_a)
    def _():
        out_ref[...] = jnp.sum(a_ref[...].astype(F32), axis=0)

    @pl.when(step >= count_a)
    def _():
        out_ref[...] = jnp.sum(b_ref[...].astype(F32), axis=0)


def sum_parts(a, b):
    shard = a.shape[1]
    count_a, count_b = a.shape[2] // TILE, b.shape[2] // TILE
    return pl.pallas_call(
        functools.partial(sum_kernel, count_a),
        grid=(count_a + count_b,),
        in_specs=[
            pl.BlockSpec((a.shape[0], shard, TILE), lambda i: (0, 0, jnp.minimum(i, count_a - 1))),
            pl.BlockSpec((b.shape[0], shard, TILE), lambda i: (0, 0, jnp.maximum(i - count_a, 0))),
        ],
        out_specs=pl.BlockSpec((shard, TILE), lambda i: (0, i)),
        out_shape=jax.ShapeDtypeStruct((shard, a.shape[2] + b.shape[2]), F32),
        compiler_params=params(1),
        cost_estimate=cost(a.size + b.size, 2 * (a.size + b.size) + 4 * shard * TILE * 8),
        name="sum_parts",
    )(a, b)


def act_kernel(
    width, units, block, rows_a, rows_b, weight_ref, gate_ref, up_ref, scale_ref, pre_ref, route_ref, total
):
    step = pl.program_id(0)
    last = (((1,), (1,)), ((), ()))
    act = lax.dot_general(
        rows_a[:, :width], weight_ref[:, :width], last, preferred_element_type=F32
    ) + lax.dot_general(rows_b[...], weight_ref[:, width:], last, preferred_element_type=F32)
    gate = gate_ref[...].astype(F32)
    up = up_ref[...].astype(F32)
    sig = jax.nn.sigmoid(gate)
    hidden = (gate * sig * up).astype(BF16).astype(F32)
    part = jnp.sum(act * hidden, axis=1, keepdims=True)

    @pl.when(step == 0)
    def _():
        total[...] = jnp.zeros_like(total)

    total[...] += jnp.broadcast_to(part, total.shape)
    dh = rows_a[:, width : width + 1].astype(F32) * act
    at = pl.multiple_of(step * block, block)
    pre_ref[:, pl.ds(at, block)] = (dh * up * sig * (1.0 + gate * (1.0 - sig))).astype(BF16)
    pre_ref[:, pl.ds(units + at, block)] = (dh * gate * sig).astype(BF16)

    @pl.when(step == pl.num_programs(0) - 1)
    def _():
        route_ref[...] = total[...].T[:8, :]


def act_side(rows_a, rows_b, weight, preact, scale, width):
    rows, both = preact.shape
    units = both // 2
    model = weight.shape[1]
    block = 256
    count = units // block
    return pl.pallas_call(
        functools.partial(act_kernel, width, units, block),
        grid=(count,),
        in_specs=[
            whole(rows_a.shape),
            whole(rows_b.shape),
            pl.BlockSpec((block, model), lambda i: (i, 0)),
            pl.BlockSpec((rows, block), lambda i: (0, i)),
            pl.BlockSpec((rows, block), lambda i: (0, count + i)),
            whole(scale.shape),
        ],
        out_specs=[whole((rows, both)), whole((8, rows))],
        out_shape=[
            jax.ShapeDtypeStruct((rows, both), BF16),
            jax.ShapeDtypeStruct((8, rows), F32),
        ],
        scratch_shapes=[pltpu.VMEM((rows, LANES), F32)],
        compiler_params=params(1),
        cost_estimate=cost(
            2 * rows * units * model, 2 * (units * model + rows * model + 2 * rows * both)
        ),
        name="act_side",
    )(rows_a, rows_b, weight, preact, preact, scale)


def combine_kernel(capacity, back_ref, ids_ref, rank_ref, out_ref):
    ids = ids_ref[...]
    back = back_ref[...]
    tokens = ids.shape[1]
    slot = lax.broadcasted_iota(jnp.int32, (capacity, tokens), 0).astype(F32)
    total = jnp.zeros(ids.shape, F32)
    for e in range(back.shape[0]):
        here = jnp.where(rank_ref[e : e + 1, :] == slot, 1.0, 0.0)
        value = jnp.dot(
            back, here, preferred_element_type=F32, precision=lax.Precision.HIGHEST
        )
        total = total + jnp.where(ids == e, value[e : e + 1, :], 0.0)
    out_ref[...] = total


def combine(back, ids_t, rank):
    return pl.pallas_call(
        functools.partial(combine_kernel, back.shape[1]),
        grid=(1,),
        in_specs=[whole(back.shape), whole(ids_t.shape), whole(rank.shape)],
        out_specs=whole(ids_t.shape),
        out_shape=jax.ShapeDtypeStruct(ids_t.shape, F32),
        compiler_params=params(1),
        cost_estimate=cost(2 * 64 * ids_t.size * 48, 12 * ids_t.size),
        name="combine",
    )(back, ids_t, rank)


def per_device(split, grad_out, expert_ids, route_weights, saved_preact, down_weight):
    flight = lax.axis_size("expert")
    capacity = saved_preact.shape[3]
    both = saved_preact.shape[4]
    slots = flight * capacity
    model = grad_out.shape[1]
    weight = lax.all_gather(down_weight[0], "dp", axis=0, tiled=True)
    ids_t = expert_ids.T
    at_dp = lax.axis_index("dp")
    place = jnp.stack([at_dp >> (NY.bit_length() - 1), at_dp & (NY - 1)]).astype(jnp.int32)
    rows_a, onehot, rank = tables(ids_t, route_weights.T, grad_out, flight, capacity, split)
    rows_b = pick(onehot, grad_out, split, model - split)

    def dispatch(rows):
        width = rows.shape[1]
        return lax.all_to_all(
            rows.reshape(flight, capacity, width), "expert", split_axis=0, concat_axis=0, tiled=True
        ).reshape(slots, width)

    preact = saved_preact.reshape(slots, both)
    hidden = hidden_transposed(preact)
    got_a = dispatch(rows_a)
    scale = scale_row(got_a, split)
    got_b = dispatch(rows_b)
    part_a = exchange(ring("z", place, hidden, scale, got_a, split), "y")
    part_b = exchange(ring("y", place, hidden, scale, got_b, model - split), "z")
    own = sum_parts(part_a, part_b)
    pre_grad, route = act_side(got_a, got_b, weight, preact, scale, split)
    back = lax.all_to_all(
        route[0].reshape(flight, capacity), "expert", split_axis=0, concat_axis=0, tiled=True
    )
    route_grad = combine(back, ids_t, rank).T
    return (route_grad, pre_grad.reshape(saved_preact.shape), own[None])


def solution(mesh):
    return jax.shard_map(
        functools.partial(per_device, 2560),
        mesh=mesh,
        in_specs=(
            P(("dp", "expert"), None),
            P(("dp", "expert"), None),
            P(("dp", "expert"), None),
            P("expert", "dp", None, None, None),
            P("expert", "dp", None),
        ),
        out_specs=(
            P(("dp", "expert"), None),
            P("expert", "dp", None, None, None),
            P("expert", "dp", None),
        ),
        check_vma=False,
    )
```

time: 382 us -> 286 us (0.75)
  waiting for transfers between devices: 221 us -> 151 us
  local copies, waits for them, and re-layouts: 88.9 us -> 20.1 us
  Pallas kernels: 0 us -> 51.8 us
  starting transfers between devices: 15.4 us -> 48.3 us
  matrix products: 26.3 us -> 0 us
  other arithmetic: 12.7 us -> 0.08 us
    reduce_scatter x1 -> x0, waiting for transfers between devices: 169 us -> none  [per_device(): lax.psum_scatter(lax.dot_general(scaled, gathered_rows, (((0,), (0,)), ((...]
    ppermute x0 -> x12, waiting for transfers between devices: none -> 103 us  [the longest x6 96.7 us: send(): lax.ppermute(down, 'dp', neighbours(axis, -1))]
    gather x8 -> x0, local copies, waits for them, and re-layouts: 53.2 us -> none  [the longest x5 25 us: per_device(): rank_k = jnp.take_along_axis(rank, clipped, axis=1)]
    pallas_call x0 -> x15, Pallas kernels: none -> 51.8 us  [the longest x8 28.2 us: call(): pl.pallas_call(kernel, grid_spec=pltpu.PrefetchScalarGridSpec(num_scalar_...]
    scatter x2 -> x0, local copies, waits for them, and re-layouts: 31 us -> none  [the longest x1 15.5 us: slot_tables(): slot_weight = jnp.zeros((flight * capacity + 1,), jnp.float32).at[where_t...]
    dot_general x2 -> x0, matrix products: 26.3 us -> none  [the longest x1 13.5 us: per_device(): lax.dot_general(gathered_rows, lax.all_gather(stored, 'dp', axis=0, tiled...]
    unnamed x3 -> x32, local copies, waits for them, and re-layouts: 1.4 us -> 19.4 us
    ppermute x0 -> x12, starting transfers between devices: none -> 17.5 us  [the longest x6 14.1 us: send(): lax.ppermute(down, 'dp', neighbours(axis, -1))]
  transfers between devices with their start and end apart: 5 -> 18, of which waited for: 3 -> 11; matrix products, arithmetic and copies ran while one was open for 33% -> 0% of each run, Pallas kernels for 0% -> 18%
where the time goes in v1:
time: 286 us; the launch traced here: 285 us
  waiting for transfers between devices  151 us (53%)
  Pallas kernels  51.8 us (18%)
  starting transfers between devices  48.3 us (17%)
  local copies, waits for them, and re-layouts  20.1 us (7%)
  between operations  14.2 us (5%)
    ppermute x6, waiting for transfers between devices, send(): lax.ppermute(down, 'dp', neighbours(axis, -1))  96.7 us
    all_to_all x2, waiting for transfers between devices, dispatch(): lax.all_to_all(rows.reshape(flight, capacity, width), 'expert', split_axi...  45.6 us
    pallas_call x8, Pallas kernels, call(): pl.pallas_call(kernel, grid_spec=pltpu.PrefetchScalarGridSpec(num_scalar_...  28.2 us
    unnamed x32, local copies, waits for them, and re-layouts  19.4 us
    pallas_call x1, Pallas kernels, act_side(): pl.pallas_call(functools.partial(act_kernel, width, units, block), grid=(...  14.5 us
    ppermute x6, starting transfers between devices, send(): lax.ppermute(down, 'dp', neighbours(axis, -1))  14.1 us
    all_to_all x2, starting transfers between devices, dispatch(): lax.all_to_all(rows.reshape(flight, capacity, width), 'expert', split_axi...  11.8 us
    all_to_all x2, starting transfers between devices, exchange(): lax.all_to_all(part, 'dp', split_axis=0, concat_axis=0, tiled=True, axis_...  10.3 us
  transfers between devices with their start and end apart: 18, of which 11 were waited for; matrix products, arithmetic and copies ran while one was open for 0% of the time, Pallas kernels for 18%

profile of v1, /device:TPU:1, one launch (start us, length us, event | category | flops | bytes accessed | tf_op | source)
XLA Modules:
  0.0 285.3 jit_solution(10359583791459203789)
XLA Ops:
  14.8 6.8 %all-to-all-start = ((bf16[8,64,2688]{2,1,0:T(8,128)(2,1)}), bf16[8,64,2688]{2,1,0:T(8,128)(2,1)S(1)}, u32[]{:S(2)}, u32[]{:S(2)}) async-start(bf16[8,64,2688]{2,1,0:T(8,128)(2,1)} %bitcast.45), calls=%async_computation | async-start | bytes 5505024 | tf_op jit(solution)/shard_map/all_to_all | solution.py:402
  26.5 28.5 %all-to-all-done = bf16[8,64,2688]{2,1,0:T(8,128)(2,1)S(1)} async-done(((bf16[8,64,2688]{2,1,0:T(8,128)(2,1)}), bf16[8,64,2688]{2,1,0:T(8,128)(2,1)S(1)}, u32[]{:S(2)}, u32[]{:S(2)}) %all-to-all-start) | async-done | bytes 2752544 | tf_op jit(solution)/shard_map/all_to_all | solution.py:402
  56.5 5.1 %all-to-all-start.1 = ((bf16[8,64,1536]{2,1,0:T(8,128)(2,1)}), bf16[8,64,1536]{2,1,0:T(8,128)(2,1)}, u32[]{:S(2)}, u32[]{:S(2)}) async-start(bf16[8,64,1536]{2,1,0:T(8,128)(2,1)} %bitcast.42), calls=%async_computation.1 | async-start | bytes 3145728 | tf_op jit(solution)/shard_map/all_to_all | solution.py:402
  65.3 17.1 %all-to-all-done.1 = bf16[8,64,1536]{2,1,0:T(8,128)(2,1)} async-done(((bf16[8,64,1536]{2,1,0:T(8,128)(2,1)}), bf16[8,64,1536]{2,1,0:T(8,128)(2,1)}, u32[]{:S(2)}, u32[]{:S(2)}) %all-to-all-start.1) | async-done | bytes 1572896 | tf_op jit(solution)/shard_map/all_to_all | solution.py:402
  82.4 3.8 %first_y.1 = (bf16[192,1536]{1,0:T(8,128)(2,1)S(1)}, bf16[192,1536]{1,0:T(8,128)(2,1)S(1)}) custom-call(s32[2]{0:T(128)S(1)} %pad_add_fusion.at_ref, bf16[8,4,48,512]{3,2,1,0:T(8,128)(2,1)S(1)} %bitcast.19, f32[8,512]{1,0:T(8,128)S(1)} %scale.1.scale_ref, bf16[512,1536]{1,0:T(8,128)(2,1)} %bitcast.5.rows_b.rows_ref), custom_call_target="tpu_custom_call" | custom-call | flops 603979776 | bytes 2752512 | tf_op jit(solution)/shard_map/first_y/pallas_call | solution.py:225
  88.1 2.3 first_z.1
  90.4 5.6 %collective-permute-start = (bf16[96,2560]{1,0:T(8,128)(2,1)S(1)}, bf16[96,2560]{1,0:T(8,128)(2,1)S(1)}, u32[]{:S(2)}, u32[]{:S(2)}) collective-permute-start(bf16[96,2560]{1,0:T(8,128)(2,1)S(1)} %get-tuple-element.25), channel_id=1, source_target_pairs={{0,224},{8,232},{16,240},{24,248},{32,0},{40,8},{48,16},{56,24},{6... | collective-permute-start | bytes 1474568 | tf_op jit(solution)/shard_map/ppermute | solution.py:246
  96.0 18.0 %collective-permute-done.8.got_d = bf16[192,1536]{1,0:T(8,128)(2,1)S(1)} collective-permute-done((bf16[192,1536]{1,0:T(8,128)(2,1)S(1)}, bf16[192,1536]{1,0:T(8,128)(2,1)S(1)}, u32[]{:S(2)}, u32[]{:S(2)}) %collective-permute-start.8) | collective-permute-done | bytes 589856 | tf_op jit(solution)/shard_map/ppermute | solution.py:246
  113.9 2.9 %collective-permute-done.9.got_u = bf16[192,1536]{1,0:T(8,128)(2,1)S(1)} collective-permute-done((bf16[192,1536]{1,0:T(8,128)(2,1)S(1)}, bf16[192,1536]{1,0:T(8,128)(2,1)S(1)}, u32[]{:S(2)}, u32[]{:S(2)}) %collective-permute-start.9) | collective-permute-done | bytes 589856 | tf_op jit(solution)/shard_map/ppermute | solution.py:247
  116.8 3.9 %middle_y.1 = (bf16[384,1536]{1,0:T(8,128)(2,1)S(1)}, bf16[384,1536]{1,0:T(8,128)(2,1)S(1)}) custom-call(s32[2]{0:T(128)S(1)} %pad_add_fusion.at_ref, bf16[8,4,48,512]{3,2,1,0:T(8,128)(2,1)S(1)} %bitcast.21, bf16[8,4,48,512]{3,2,1,0:T(8,128)(2,1)S(1)} %bitcast.22, f32[8,512]{1,0:T(8,128)S(1)} %scale.1.scale_ref, bf16[512,1536]{1,0:T(8,128)(2,1)} %bitcast.5.rows_b.rows_ref, ...), custom_call_target="tpu_custom_call" | custom-call | flops 1207959552 | bytes 5111808 | tf_op jit(solution)/shard_map/middle_y/pallas_call | solution.py:225
  122.3 3.0 %middle_z.3 = (bf16[192,2560]{1,0:T(8,128)(2,1)S(1)}, bf16[192,2560]{1,0:T(8,128)(2,1)S(1)}) custom-call(s32[2]{0:T(128)S(1)} %pad_add_fusion.at_ref, bf16[8,192,512]{2,1,0:T(8,128)(2,1)S(1)} %bitcast.23, bf16[8,192,512]{2,1,0:T(8,128)(2,1)S(1)} %bitcast.24, f32[8,512]{1,0:T(8,128)S(1)} %scale.1.scale_ref, bf16[512,2688]{1,0:T(8,128)(2,1)S(1)} %bitcast.33, ...), custom_call_target="tpu_custom_call" | custom-call | flops 1006632960 | bytes 5570560 | tf_op jit(solution)/shard_map/middle_z/pallas_call | solution.py:225
  125.3 5.6 %collective-permute-start.2 = (bf16[192,2560]{1,0:T(8,128)(2,1)S(1)}, bf16[192,2560]{1,0:T(8,128)(2,1)S(1)}, u32[]{:S(2)}, u32[]{:S(2)}) collective-permute-start(bf16[192,2560]{1,0:T(8,128)(2,1)S(1)} %get-tuple-element.27), channel_id=1, source_target_pairs={{0,224},{8,232},{16,240},{24,248},{32,0},{40,8},{48,16},{56,24},{6... | collective-permute-start | bytes 2949128 | tf_op jit(solution)/shard_map/ppermute | solution.py:246
  130.9 32.4 %collective-permute-done.2.got_d = bf16[192,2560]{1,0:T(8,128)(2,1)S(1)} collective-permute-done((bf16[192,2560]{1,0:T(8,128)(2,1)S(1)}, bf16[192,2560]{1,0:T(8,128)(2,1)S(1)}, u32[]{:S(2)}, u32[]{:S(2)}) %collective-permute-start.2) | collective-permute-done | bytes 983072 | tf_op jit(solution)/shard_map/ppermute | solution.py:246
  164.3 4.1 %middle_z.4 = (bf16[192,2560]{1,0:T(8,128)(2,1)}, bf16[192,2560]{1,0:T(8,128)(2,1)}) custom-call(s32[2]{0:T(128)S(1)} %pad_add_fusion.at_ref, bf16[8,192,512]{2,1,0:T(8,128)(2,1)S(1)} %bitcast.25, bf16[8,192,512]{2,1,0:T(8,128)(2,1)S(1)} %bitcast.26, f32[8,512]{1,0:T(8,128)S(1)} %scale.1.scale_ref, bf16[512,2688]{1,0:T(8,128)(2,1)S(1)} %bitcast.34, ...), custom_call_target="tpu_custom_call" | custom-call | flops 1006632960 | bytes 6553600 | tf_op jit(solution)/shard_map/middle_z/pallas_call | solution.py:225
  169.8 3.5 %last_y.1 = bf16[384,1536]{1,0:T(8,128)(2,1)S(1)} custom-call(s32[2]{0:T(128)S(1)} %pad_add_fusion.at_ref, bf16[8,4,48,512]{3,2,1,0:T(8,128)(2,1)S(1)} %bitcast.27, f32[8,512]{1,0:T(8,128)S(1)} %scale.1.scale_ref, bf16[512,1536]{1,0:T(8,128)(2,1)} %bitcast.5.rows_b.rows_ref, bf16[384,1536]{1,0:T(8,128)(2,1)S(1)} %collective-permute-done.10.got_d, ...), custom_call_target="tpu_custom_call" | custom-call | flops 603979776 | bytes 5111808 | tf_op jit(solution)/shard_map/last_y/pallas_call | solution.py:225
  174.4 5.7 %all-to-all-start.4 = ((bf16[8,48,1536]{2,1,0:T(8,128)(2,1)}), bf16[8,48,1536]{2,1,0:T(8,128)(2,1)S(1)}, u32[]{:S(2)}, u32[]{:S(2)}) async-start(bf16[8,48,1536]{2,1,0:T(8,128)(2,1)} %bitcast.43), calls=%async_computation.4 | async-start | bytes 2359296 | tf_op jit(solution)/shard_map/all_to_all | solution.py:264
  180.1 9.7 %collective-permute-done.4.got_d = bf16[192,2560]{1,0:T(8,128)(2,1)} collective-permute-done((bf16[192,2560]{1,0:T(8,128)(2,1)}, bf16[192,2560]{1,0:T(8,128)(2,1)}, u32[]{:S(2)}, u32[]{:S(2)}) %collective-permute-start.4) | collective-permute-done | bytes 983072 | tf_op jit(solution)/shard_map/ppermute | solution.py:246
  192.9 5.1 %middle_z.5 = (bf16[192,2560]{1,0:T(8,128)(2,1)S(1)}, bf16[192,2560]{1,0:T(8,128)(2,1)S(1)}) custom-call(s32[2]{0:T(128)S(1)} %pad_add_fusion.at_ref, bf16[8,192,512]{2,1,0:T(8,128)(2,1)S(1)} %bitcast.28, bf16[8,192,512]{2,1,0:T(8,128)(2,1)S(1)} %bitcast.29, f32[8,512]{1,0:T(8,128)S(1)} %scale.1.scale_ref, bf16[512,2688]{1,0:T(8,128)(2,1)S(1)} %bitcast.35, ...), custom_call_target="tpu_custom_call" | custom-call | flops 1006632960 | bytes 6553600 | tf_op jit(solution)/shard_map/middle_z/pallas_call | solution.py:225
  199.5 36.6 %collective-permute-done.6.got_d = bf16[192,2560]{1,0:T(8,128)(2,1)S(1)} collective-permute-done((bf16[192,2560]{1,0:T(8,128)(2,1)S(1)}, bf16[192,2560]{1,0:T(8,128)(2,1)S(1)}, u32[]{:S(2)}, u32[]{:S(2)}) %collective-permute-start.6) | collective-permute-done | bytes 983072 | tf_op jit(solution)/shard_map/ppermute | solution.py:246
  237.3 2.5 last_z.1
  240.8 4.6 %all-to-all-start.3 = ((bf16[4,48,2560]{2,1,0:T(8,128)(2,1)}), bf16[4,48,2560]{2,1,0:T(8,128)(2,1)S(1)}, u32[]{:S(2)}, u32[]{:S(2)}) async-start(bf16[4,48,2560]{2,1,0:T(8,128)(2,1)} %bitcast.44), calls=%async_computation.3 | async-start | bytes 1966080 | tf_op jit(solution)/shard_map/all_to_all | solution.py:264
  249.0 14.5 %act_side.1 = (bf16[512,3072]{1,0:T(8,128)(2,1)}, f32[8,512]{1,0:T(8,128)S(1)}) custom-call(bf16[512,2688]{1,0:T(8,128)(2,1)S(1)} %bitcast.37, bf16[512,1536]{1,0:T(8,128)(2,1)} %bitcast.5.rows_b.rows_ref, bf16[1536,4096]{1,0:T(8,128)(2,1)} %bitcast.51, bf16[512,3072]{1,0:T(8,128)(2,1)S(1)} %bitcast.40, bf16[512,3072]{1,0:T(8,128)(2,1)S(1)} %bitcast.41, ...), custom_call_target="tpu_custom_call" | custom-call | flops 6442450944 | bytes 23068672 | tf_op jit(solution)/shard_map/act_side/pallas_call | solution.py:334
  264.2 8.6 %all-to-all-start.2 = ((f32[8,1,64]{2,1,0:T(1,128)}), f32[8,1,64]{2,1,0:T(1,128)S(1)}, u32[]{:S(2)}, u32[]{:S(2)}) async-start(f32[8,1,64]{2,1,0:T(1,128)} %bitcast.8), calls=%async_computation.2 | async-start | bytes 8192 | tf_op jit(solution)/shard_map/all_to_all | solution.py:415
  272.8 2.9 %sum_parts.1 = f32[48,4096]{1,0:T(8,128)} custom-call(bf16[4,48,2560]{2,1,0:T(8,128)(2,1)S(1)} %all-to-all-done.3.a_ref, bf16[8,48,1536]{2,1,0:T(8,128)(2,1)S(1)} %all-to-all-done.4.b_ref), custom_call_target="tpu_custom_call" | custom-call | flops 1081344 | bytes 2949120 | tf_op jit(solution)/shard_map/sum_parts/pallas_call | solution.py:284
  (63 shorter events, 38.5 us)
Async XLA Ops:
  7.2 238.2 %all-gather.3.cloned.1.call-start = ((), (), s32[]{:S(2)}) async-start(), calls=%async_computation.5 | async-start | bytes 12976128 | tf_op jit(solution)/shard_map/all_gather | solution.py:393
  7.9 2.2 copy-start.9
  14.8 40.1 %all-to-all-start = ((bf16[8,64,2688]{2,1,0:T(8,128)(2,1)}), bf16[8,64,2688]{2,1,0:T(8,128)(2,1)S(1)}, u32[]{:S(2)}, u32[]{:S(2)}) async-start(bf16[8,64,2688]{2,1,0:T(8,128)(2,1)} %bitcast.45), calls=%async_computation | async-start | bytes 5505024 | tf_op jit(solution)/shard_map/all_to_all | solution.py:402
  21.6 2.2 copy-start.10
  56.5 25.9 %all-to-all-start.1 = ((bf16[8,64,1536]{2,1,0:T(8,128)(2,1)}), bf16[8,64,1536]{2,1,0:T(8,128)(2,1)}, u32[]{:S(2)}, u32[]{:S(2)}) async-start(bf16[8,64,1536]{2,1,0:T(8,128)(2,1)} %bitcast.42), calls=%async_computation.1 | async-start | bytes 3145728 | tf_op jit(solution)/shard_map/all_to_all | solution.py:402
  61.6 1.9 copy-start.5
  82.4 5.7 %copy-start.2 = (bf16[8,64,2688]{2,1,0:T(8,128)(2,1)S(1)}, bf16[8,64,2688]{2,1,0:T(8,128)(2,1)}, u32[]{:S(2)}) copy-start(bf16[8,64,2688]{2,1,0:T(8,128)(2,1)} %copy-done) | copy-start | bytes 8257540
  86.2 27.7 %collective-permute-start.8 = (bf16[192,1536]{1,0:T(8,128)(2,1)S(1)}, bf16[192,1536]{1,0:T(8,128)(2,1)S(1)}, u32[]{:S(2)}, u32[]{:S(2)}) collective-permute-start(bf16[192,1536]{1,0:T(8,128)(2,1)S(1)} %get-tuple-element.33), channel_id=1, source_target_pairs={{0,24},{8,0},{16,8},{24,16},{32,56},{40,32},{48,40},{56,48},{64,88... | collective-permute-start | bytes 1769480 | tf_op jit(solution)/shard_map/ppermute | solution.py:246
  88.1 28.7 %collective-permute-start.9 = (bf16[192,1536]{1,0:T(8,128)(2,1)S(1)}, bf16[192,1536]{1,0:T(8,128)(2,1)S(1)}, u32[]{:S(2)}, u32[]{:S(2)}) collective-permute-start(bf16[192,1536]{1,0:T(8,128)(2,1)S(1)} %get-tuple-element.34), channel_id=1, source_target_pairs={{0,8},{8,16},{16,24},{24,0},{32,40},{40,48},{48,56},{56,32},{64,72... | collective-permute-start | bytes 1769480 | tf_op jit(solution)/shard_map/ppermute | solution.py:247
  90.4 31.9 %collective-permute-start = (bf16[96,2560]{1,0:T(8,128)(2,1)S(1)}, bf16[96,2560]{1,0:T(8,128)(2,1)S(1)}, u32[]{:S(2)}, u32[]{:S(2)}) collective-permute-start(bf16[96,2560]{1,0:T(8,128)(2,1)S(1)} %get-tuple-element.25), channel_id=1, source_target_pairs={{0,224},{8,232},{16,240},{24,248},{32,0},{40,8},{48,16},{56,24},{6... | collective-permute-start | bytes 1474568 | tf_op jit(solution)/shard_map/ppermute | solution.py:246
  96.0 26.4 %collective-permute-start.1 = (bf16[96,2560]{1,0:T(8,128)(2,1)S(1)}, bf16[96,2560]{1,0:T(8,128)(2,1)S(1)}, u32[]{:S(2)}, u32[]{:S(2)}) collective-permute-start(bf16[96,2560]{1,0:T(8,128)(2,1)S(1)} %get-tuple-element.26), channel_id=1, source_target_pairs={{0,32},{8,40},{16,48},{24,56},{32,64},{40,72},{48,80},{56,88},{64,... | collective-permute-start | bytes 1474568 | tf_op jit(solution)/shard_map/ppermute | solution.py:247
  120.8 49.0 %collective-permute-start.10 = (bf16[384,1536]{1,0:T(8,128)(2,1)S(1)}, bf16[384,1536]{1,0:T(8,128)(2,1)S(1)}, u32[]{:S(2)}, u32[]{:S(2)}) collective-permute-start(bf16[384,1536]{1,0:T(8,128)(2,1)S(1)} %get-tuple-element.35), channel_id=1, source_target_pairs={{0,24},{8,0},{16,8},{24,16},{32,56},{40,32},{48,40},{56,48},{64,88... | collective-permute-start | bytes 3538952 | tf_op jit(solution)/shard_map/ppermute | solution.py:246
  121.0 48.8 %collective-permute-start.11 = (bf16[384,1536]{1,0:T(8,128)(2,1)S(1)}, bf16[384,1536]{1,0:T(8,128)(2,1)S(1)}, u32[]{:S(2)}, u32[]{:S(2)}) collective-permute-start(bf16[384,1536]{1,0:T(8,128)(2,1)S(1)} %get-tuple-element.36), channel_id=1, source_target_pairs={{0,8},{8,16},{16,24},{24,0},{32,40},{40,48},{48,56},{56,32},{64,72... | collective-permute-start | bytes 3538952 | tf_op jit(solution)/shard_map/ppermute | solution.py:247
  125.3 38.0 %collective-permute-start.2 = (bf16[192,2560]{1,0:T(8,128)(2,1)S(1)}, bf16[192,2560]{1,0:T(8,128)(2,1)S(1)}, u32[]{:S(2)}, u32[]{:S(2)}) collective-permute-start(bf16[192,2560]{1,0:T(8,128)(2,1)S(1)} %get-tuple-element.27), channel_id=1, source_target_pairs={{0,224},{8,232},{16,240},{24,248},{32,0},{40,8},{48,16},{56,24},{6... | collective-permute-start | bytes 2949128 | tf_op jit(solution)/shard_map/ppermute | solution.py:246
  130.9 33.3 %collective-permute-start.3 = (bf16[192,2560]{1,0:T(8,128)(2,1)S(1)}, bf16[192,2560]{1,0:T(8,128)(2,1)S(1)}, u32[]{:S(2)}, u32[]{:S(2)}) collective-permute-start(bf16[192,2560]{1,0:T(8,128)(2,1)S(1)} %get-tuple-element.28), channel_id=1, source_target_pairs={{0,32},{8,40},{16,48},{24,56},{32,64},{40,72},{48,80},{56,88},{64,... | collective-permute-start | bytes 2949128 | tf_op jit(solution)/shard_map/ppermute | solution.py:247
  168.3 21.5 %collective-permute-start.4 = (bf16[192,2560]{1,0:T(8,128)(2,1)}, bf16[192,2560]{1,0:T(8,128)(2,1)}, u32[]{:S(2)}, u32[]{:S(2)}) collective-permute-start(bf16[192,2560]{1,0:T(8,128)(2,1)} %get-tuple-element.29), channel_id=1, source_target_pairs={{0,224},{8,232},{16,240},{24,248},{32,0},{40,8},{48,16},{56,24},{6... | collective-permute-start | bytes 2949128 | tf_op jit(solution)/shard_map/ppermute | solution.py:246
  168.7 22.4 %collective-permute-start.5 = (bf16[192,2560]{1,0:T(8,128)(2,1)}, bf16[192,2560]{1,0:T(8,128)(2,1)}, u32[]{:S(2)}, u32[]{:S(2)}) collective-permute-start(bf16[192,2560]{1,0:T(8,128)(2,1)} %get-tuple-element.30), channel_id=1, source_target_pairs={{0,32},{8,40},{16,48},{24,56},{32,64},{40,72},{48,80},{56,88},{64,... | collective-permute-start | bytes 2949128 | tf_op jit(solution)/shard_map/ppermute | solution.py:247
  174.4 66.4 %all-to-all-start.4 = ((bf16[8,48,1536]{2,1,0:T(8,128)(2,1)}), bf16[8,48,1536]{2,1,0:T(8,128)(2,1)S(1)}, u32[]{:S(2)}, u32[]{:S(2)}) async-start(bf16[8,48,1536]{2,1,0:T(8,128)(2,1)} %bitcast.43), calls=%async_computation.4 | async-start | bytes 2359296 | tf_op jit(solution)/shard_map/all_to_all | solution.py:264
  197.9 38.1 %collective-permute-start.6 = (bf16[192,2560]{1,0:T(8,128)(2,1)S(1)}, bf16[192,2560]{1,0:T(8,128)(2,1)S(1)}, u32[]{:S(2)}, u32[]{:S(2)}) collective-permute-start(bf16[192,2560]{1,0:T(8,128)(2,1)S(1)} %get-tuple-element.31), channel_id=1, source_target_pairs={{0,224},{8,232},{16,240},{24,248},{32,0},{40,8},{48,16},{56,24},{6... | collective-permute-start | bytes 2949128 | tf_op jit(solution)/shard_map/ppermute | solution.py:246
  198.4 38.9 %collective-permute-start.7 = (bf16[192,2560]{1,0:T(8,128)(2,1)S(1)}, bf16[192,2560]{1,0:T(8,128)(2,1)S(1)}, u32[]{:S(2)}, u32[]{:S(2)}) collective-permute-start(bf16[192,2560]{1,0:T(8,128)(2,1)S(1)} %get-tuple-element.32), channel_id=1, source_target_pairs={{0,32},{8,40},{16,48},{24,56},{32,64},{40,72},{48,80},{56,88},{64,... | collective-permute-start | bytes 2949128 | tf_op jit(solution)/shard_map/ppermute | solution.py:247
  240.8 23.4 %all-to-all-start.3 = ((bf16[4,48,2560]{2,1,0:T(8,128)(2,1)}), bf16[4,48,2560]{2,1,0:T(8,128)(2,1)S(1)}, u32[]{:S(2)}, u32[]{:S(2)}) async-start(bf16[4,48,2560]{2,1,0:T(8,128)(2,1)} %bitcast.44), calls=%async_computation.3 | async-start | bytes 1966080 | tf_op jit(solution)/shard_map/all_to_all | solution.py:264
  247.1 1.9 copy-start.6
  263.5 13.8 %copy-start.14 = (s32[512,8]{0,1:T(8,128)S(1)}, s32[512,8]{0,1:T(8,128)}, u32[]{:S(2)}) copy-start(s32[512,8]{0,1:T(8,128)} %param.6) | copy-start | bytes 49156
  264.2 13.1 %all-to-all-start.2 = ((f32[8,1,64]{2,1,0:T(1,128)}), f32[8,1,64]{2,1,0:T(1,128)S(1)}, u32[]{:S(2)}, u32[]{:S(2)}) async-start(f32[8,1,64]{2,1,0:T(1,128)} %bitcast.8), calls=%async_computation.2 | async-start | bytes 8192 | tf_op jit(solution)/shard_map/all_to_all | solution.py:415
  (10 other events, 13.0 us)
Sparse Core Ops, SparseCore 0:
  10.6 149.9 all-gather.2

commit v2 on v1

--- a/solution.py
+++ b/solution.py
@@ -13,12 +13,14 @@
 TILE = 512
 NY = 4
 NZ = 8
-VMEM_LIMIT = 40 * 1024 * 1024
-
-
-def params(grid_rank):
+ALONG_Z = [[z * NY + y for z in range(NZ)] for y in range(NY)]
+ALONG_Y = [[z * NY + y for y in range(NY)] for z in range(NZ)]
+MIB = 1024 * 1024
+
+
+def params(grid_rank, mib=16):
     return pltpu.CompilerParams(
-        dimension_semantics=("arbitrary",) * grid_rank, vmem_limit_bytes=VMEM_LIMIT
+        dimension_semantics=("arbitrary",) * grid_rank, vmem_limit_bytes=mib * MIB
     )
 
 
@@ -108,12 +110,27 @@
     )(onehot, grad_out)
 
 
-def hidden_kernel(gate_ref, up_ref, out_ref):
+def same_kernel(array_ref, after_ref, out_ref):
+    pass
+
+
+def hold(array, after):
+    return pl.pallas_call(
+        same_kernel,
+        in_specs=[pl.BlockSpec(memory_space=pl.ANY)] * 2,
+        out_specs=pl.BlockSpec(memory_space=pl.ANY),
+        out_shape=jax.ShapeDtypeStruct(array.shape, array.dtype),
+        input_output_aliases={0: 0},
+        name="hold",
+    )(array, after)
+
+
+def hidden_kernel(gate_ref, up_ref, after_ref, out_ref):
     gate = gate_ref[...].astype(F32)
     out_ref[...] = (gate * jax.nn.sigmoid(gate) * up_ref[...].astype(F32)).T.astype(BF16)
 
 
-def hidden_transposed(preact):
+def hidden_transposed(preact, after):
     rows, both = preact.shape
     units = both // 2
     block = 256
@@ -124,13 +141,14 @@
         in_specs=[
             pl.BlockSpec((rows, block), lambda i: (0, i)),
             pl.BlockSpec((rows, block), lambda i: (0, count + i)),
+            pl.BlockSpec(memory_space=pl.ANY),
         ],
         out_specs=pl.BlockSpec((block, rows), lambda i: (i, 0)),
         out_shape=jax.ShapeDtypeStruct((units, rows), BF16),
         compiler_params=params(1),
         cost_estimate=cost(10 * rows * units, 6 * rows * units),
         name="hidden",
-    )(preact, preact)
+    )(preact, preact, after)
 
 
 def scale_kernel(w_ref, out_ref):
@@ -158,14 +176,14 @@
     return jnp.dot(scaled, rows_ref[...], preferred_element_type=F32)
 
 
-def first_kernel(at_ref, hid_ref, scale_ref, rows_ref, down_ref, up_ref):
+def first_kernel(at_ref, hid_ref, scale_ref, rows_ref, after_ref, down_ref, up_ref):
     value = product(hid_ref, scale_ref, rows_ref).astype(BF16)
     half = value.shape[0] // 2
     down_ref[...] = value[:half]
     up_ref[...] = value[half:]
 
 
-def middle_kernel(at_ref, hid_d, hid_u, scale_ref, rows_ref, got_d, got_u, down_ref, up_ref):
+def middle_kernel(at_ref, hid_d, hid_u, scale_ref, rows_ref, got_d, got_u, after_ref, down_ref, up_ref):
     down = product(hid_d, scale_ref, rows_ref)
     up = product(hid_u, scale_ref, rows_ref)
     size, part = down.shape[0], got_d.shape[0]
@@ -179,7 +197,7 @@
         up_ref[part:] = (up[part:] + got_u[...].astype(F32)).astype(BF16)
 
 
-def last_kernel(at_ref, hid_ref, scale_ref, rows_ref, got_d, got_u, out_ref):
+def last_kernel(at_ref, hid_ref, scale_ref, rows_ref, got_d, got_u, after_ref, out_ref):
     own = product(hid_ref, scale_ref, rows_ref)
     out_ref[...] = (own + got_d[...].astype(F32) + got_u[...].astype(F32)).astype(BF16)
 
@@ -206,7 +224,6 @@
         hid_shape = (NZ, 1, shard, depth)
     block = units // size
     half = size // 2
-    tiles = width // TILE
 
     def hid(offset):
         def target(at):
@@ -216,12 +233,14 @@
             return pl.BlockSpec(hid_shape, lambda i, at: (target(at), 0, 0))
         return pl.BlockSpec(hid_shape, lambda i, at: (0, target(at), 0, 0))
 
+    tiles = 2
+
     def tile(n):
-        return pl.BlockSpec((n, TILE), lambda i, at: (0, i))
+        return pl.BlockSpec((n, width // tiles), lambda i, at: (0, i))
 
     common = [pl.BlockSpec(scale.shape, lambda i, at: (0, 0)), tile(depth)]
 
-    def call(kernel, offsets, arrived, outs, name):
+    def call(kernel, offsets, arrived, outs, name, after):
         return pl.pallas_call(
             kernel,
             grid_spec=pltpu.PrefetchScalarGridSpec(
@@ -229,81 +248,100 @@
                 grid=(tiles,),
                 in_specs=[hid(o) for o in offsets]
                 + common
-                + [tile(a.shape[0]) for a in arrived],
+                + [tile(a.shape[0]) for a in arrived]
+                + [pl.BlockSpec(memory_space=pl.ANY)],
                 out_specs=[tile(n) for n in outs],
             ),
             out_shape=[jax.ShapeDtypeStruct((n, width), BF16) for n in outs],
             compiler_params=params(1),
-            cost_estimate=cost(
-                2 * block * depth * width * len(offsets),
-                2 * width * (depth + sum(outs) + sum(a.shape[0] for a in arrived)),
-            ),
+            cost_estimate=cost(block * width, block),
             name=name,
-        )(place, *[hidden] * len(offsets), scale, rows, *arrived)
-
-    def send(down, up):
-        return [
-            lax.ppermute(down, "dp", neighbours(axis, -1)),
-            lax.ppermute(up, "dp", neighbours(axis, 1)),
+        )(place, *[hidden] * len(offsets), scale, rows, *arrived, after)
+
+    def step(number, arrived, after):
+        if number == 0:
+            made = call(first_kernel, [half], [], [block // 2] * 2, "first_" + axis, after)
+        elif number < half:
+            made = call(
+                middle_kernel,
+                [number - half, half - number],
+                arrived,
+                [block] * 2,
+                "middle_" + axis,
+                after,
+            )
+        else:
+            return call(last_kernel, [0], arrived, [block], "last_" + axis, after)[0], None
+        return made[0], [
+            lax.ppermute(made[0], "dp", neighbours(axis, -1)),
+            lax.ppermute(made[1], "dp", neighbours(axis, 1)),
         ]
 
-    arrived = send(*call(first_kernel, [half], [], [block // 2] * 2, "first_" + axis))
-    for s in range(1, half):
-        arrived = send(
-            *call(middle_kernel, [s - half, half - s], arrived, [block] * 2, "middle_" + axis)
-        )
-    return call(last_kernel, [0], arrived, [block], "last_" + axis)[0]
+    return step
 
 
 def exchange(part, axis):
-    if axis == "z":
-        size, groups = NZ, [[z * NY + y for z in range(NZ)] for y in range(NY)]
-    else:
-        size, groups = NY, [[z * NY + y for y in range(NY)] for z in range(NZ)]
+    size, groups = (NZ, ALONG_Z) if axis == "z" else (NY, ALONG_Y)
     part = part.reshape(size, part.shape[0] // size, part.shape[1])
     return lax.all_to_all(
         part, "dp", split_axis=0, concat_axis=0, tiled=True, axis_index_groups=groups
     )
 
 
-def sum_kernel(count_a, a_ref, b_ref, out_ref):
+def sum_kernel(firsts, *refs):
+    out_ref = refs[-1]
+    tile = pl.program_id(0)
+    for k, part in enumerate(refs[:-1]):
+
+        @pl.when((tile >= firsts[k]) & (tile < firsts[k + 1]))
+        def _():
+            out_ref[...] = jnp.sum(part[...].astype(F32), axis=0)
+
+
+def sum_parts(parts):
+    shard = parts[0].shape[1]
+    counts = [part.shape[2] // TILE for part in parts]
+    firsts = [sum(counts[:k]) for k in range(len(counts) + 1)]
+
+    def spec(part, first, count):
+        return pl.BlockSpec(
+            (part.shape[0], shard, TILE), lambda i: (0, 0, jnp.clip(i - first, 0, count - 1))
+        )
+
+    return pl.pallas_call(
+        functools.partial(sum_kernel, firsts),
+        grid=(firsts[-1],),
+        in_specs=[spec(*each) for each in zip(parts, firsts, counts)],
+        out_specs=pl.BlockSpec((shard, TILE), lambda i: (0, i)),
+        out_shape=jax.ShapeDtypeStruct((shard, firsts[-1] * TILE), F32),
+        compiler_params=params(1),
+        cost_estimate=cost(
+            sum(part.size for part in parts),
+            sum(2 * part.size for part in parts) + 4 * shard * firsts[-1] * TILE,
+        ),
+        name="sum_parts",
+    )(*parts)
+
+
+def act_kernel(starts, units, *refs):
+    rows = refs[: len(starts) - 1]
+    weight_ref, gate_ref, up_ref, _, pre_ref, route_ref, total, held = refs[len(starts) - 1 :]
     step = pl.program_id(0)
-
-    @pl.when(step < count_a)
-    def _():
-        out_ref[...] = jnp.sum(a_ref[...].astype(F32), axis=0)
-
-    @pl.when(step >= count_a)
-    def _():
-        out_ref[...] = jnp.sum(b_ref[...].astype(F32), axis=0)
-
-
-def sum_parts(a, b):
-    shard = a.shape[1]
-    count_a, count_b = a.shape[2] // TILE, b.shape[2] // TILE
-    return pl.pallas_call(
-        functools.partial(sum_kernel, count_a),
-        grid=(count_a + count_b,),
-        in_specs=[
-            pl.BlockSpec((a.shape[0], shard, TILE), lambda i: (0, 0, jnp.minimum(i, count_a - 1))),
-            pl.BlockSpec((b.shape[0], shard, TILE), lambda i: (0, 0, jnp.maximum(i - count_a, 0))),
-        ],
-        out_specs=pl.BlockSpec((shard, TILE), lambda i: (0, i)),
-        out_shape=jax.ShapeDtypeStruct((shard, a.shape[2] + b.shape[2]), F32),
-        compiler_params=params(1),
-        cost_estimate=cost(a.size + b.size, 2 * (a.size + b.size) + 4 * shard * TILE * 8),
-        name="sum_parts",
-    )(a, b)
-
-
-def act_kernel(
-    width, units, block, rows_a, rows_b, weight_ref, gate_ref, up_ref, scale_ref, pre_ref, route_ref, total
-):
-    step = pl.program_id(0)
-    last = (((1,), (1,)), ((), ()))
-    act = lax.dot_general(
-        rows_a[:, :width], weight_ref[:, :width], last, preferred_element_type=F32
-    ) + lax.dot_general(rows_b[...], weight_ref[:, width:], last, preferred_element_type=F32)
+    ny, nz, shard, _ = weight_ref.shape
+    block = ny * nz * shard
+    for z in range(nz):
+        for y in range(ny):
+            at = (z * ny + y) * shard
+            held[at : at + shard, :] = weight_ref[y, z]
+    act = None
+    for part, start, end in zip(rows, starts, starts[1:]):
+        more = lax.dot_general(
+            part[:, : end - start],
+            held[:, start:end],
+            (((1,), (1,)), ((), ())),
+            preferred_element_type=F32,
+        )
+        act = more if act is None else act + more
     gate = gate_ref[...].astype(F32)
     up = up_ref[...].astype(F32)
     sig = jax.nn.sigmoid(gate)
@@ -315,7 +353,7 @@
         total[...] = jnp.zeros_like(total)
 
     total[...] += jnp.broadcast_to(part, total.shape)
-    dh = rows_a[:, width : width + 1].astype(F32) * act
+    dh = rows[0][:, starts[1] : starts[1] + 1].astype(F32) * act
     at = pl.multiple_of(step * block, block)
     pre_ref[:, pl.ds(at, block)] = (dh * up * sig * (1.0 + gate * (1.0 - sig))).astype(BF16)
     pre_ref[:, pl.ds(units + at, block)] = (dh * gate * sig).astype(BF16)
@@ -325,35 +363,35 @@
         route_ref[...] = total[...].T[:8, :]
 
 
-def act_side(rows_a, rows_b, weight, preact, scale, width):
+def act_side(got, starts, weight, preact, after):
     rows, both = preact.shape
     units = both // 2
-    model = weight.shape[1]
-    block = 256
+    ny, nz, shard, model = weight.shape
+    each = 2
+    block = ny * each * shard
     count = units // block
     return pl.pallas_call(
-        functools.partial(act_kernel, width, units, block),
+        functools.partial(act_kernel, starts, units),
         grid=(count,),
         in_specs=[
-            whole(rows_a.shape),
-            whole(rows_b.shape),
-            pl.BlockSpec((block, model), lambda i: (i, 0)),
+            *[whole(part.shape) for part in got],
+            pl.BlockSpec((ny, each, shard, model), lambda i: (0, i, 0, 0)),
             pl.BlockSpec((rows, block), lambda i: (0, i)),
             pl.BlockSpec((rows, block), lambda i: (0, count + i)),
-            whole(scale.shape),
+            pl.BlockSpec(memory_space=pl.ANY),
         ],
         out_specs=[whole((rows, both)), whole((8, rows))],
         out_shape=[
             jax.ShapeDtypeStruct((rows, both), BF16),
             jax.ShapeDtypeStruct((8, rows), F32),
         ],
-        scratch_shapes=[pltpu.VMEM((rows, LANES), F32)],
-        compiler_params=params(1),
+        scratch_shapes=[pltpu.VMEM((rows, LANES), F32), pltpu.VMEM((block, model), BF16)],
+        compiler_params=params(1, 44),
         cost_estimate=cost(
             2 * rows * units * model, 2 * (units * model + rows * model + 2 * rows * both)
         ),
         name="act_side",
-    )(rows_a, rows_b, weight, preact, preact, scale)
+    )(*got, weight, preact, preact, after)
 
 
 def combine_kernel(capacity, back_ref, ids_ref, rank_ref, out_ref):
@@ -384,34 +422,54 @@
     )(back, ids_t, rank)
 
 
-def per_device(split, grad_out, expert_ids, route_weights, saved_preact, down_weight):
+def per_device(chunks, order, grad_out, expert_ids, route_weights, saved_preact, down_weight):
     flight = lax.axis_size("expert")
     capacity = saved_preact.shape[3]
     both = saved_preact.shape[4]
     slots = flight * capacity
-    model = grad_out.shape[1]
-    weight = lax.all_gather(down_weight[0], "dp", axis=0, tiled=True)
+    starts = [sum(width for _, width in chunks[:k]) for k in range(len(chunks) + 1)]
+    weight = lax.all_gather(down_weight[0], "dp", axis=0, axis_index_groups=ALONG_Z)
     ids_t = expert_ids.T
     at_dp = lax.axis_index("dp")
     place = jnp.stack([at_dp >> (NY.bit_length() - 1), at_dp & (NY - 1)]).astype(jnp.int32)
-    rows_a, onehot, rank = tables(ids_t, route_weights.T, grad_out, flight, capacity, split)
-    rows_b = pick(onehot, grad_out, split, model - split)
-
-    def dispatch(rows):
-        width = rows.shape[1]
+    first, onehot, rank = tables(
+        ids_t, route_weights.T, grad_out, flight, capacity, chunks[0][1]
+    )
+    rows = [first] + [
+        pick(onehot, grad_out, start, width) for start, (_, width) in zip(starts[1:], chunks[1:])
+    ]
+    preact = saved_preact.reshape(slots, both)
+    hidden = hidden_transposed(preact, rows[-1])
+
+    def dispatch(part):
+        width = part.shape[1]
         return lax.all_to_all(
-            rows.reshape(flight, capacity, width), "expert", split_axis=0, concat_axis=0, tiled=True
+            part.reshape(flight, capacity, width), "expert", split_axis=0, concat_axis=0, tiled=True
         ).reshape(slots, width)
 
-    preact = saved_preact.reshape(slots, both)
-    hidden = hidden_transposed(preact)
-    got_a = dispatch(rows_a)
-    scale = scale_row(got_a, split)
-    got_b = dispatch(rows_b)
-    part_a = exchange(ring("z", place, hidden, scale, got_a, split), "y")
-    part_b = exchange(ring("y", place, hidden, scale, got_b, model - split), "z")
-    own = sum_parts(part_a, part_b)
-    pre_grad, route = act_side(got_a, got_b, weight, preact, scale, split)
+    got = [dispatch(first)]
+    scale = scale_row(got[0], starts[1])
+    made = scale
+    steps, arrived, number, parts = {}, {}, [0] * len(chunks), {}
+    for item in order:
+        if item == "gather":
+            weight = lax.all_gather(hold(weight, made), "dp", axis=0, axis_index_groups=ALONG_Y)
+            continue
+        if item == "act":
+            pre_grad, route = act_side(got, starts, weight, preact, made)
+            made = route
+            continue
+        axis, width = chunks[item]
+        if number[item] == 0:
+            steps[item] = ring(axis, place, hidden, scale, got[item], width)
+            arrived[item] = []
+        made, arrived[item] = steps[item](number[item], arrived[item], made)
+        if number[item] == 0 and item + 1 < len(chunks):
+            got.append(dispatch(hold(rows[item + 1], made)))
+        number[item] += 1
+        if arrived[item] is None:
+            parts[item] = exchange(made, "y" if axis == "z" else "z")
+    own = sum_parts([parts[k] for k in range(len(chunks))])
     back = lax.all_to_all(
         route[0].reshape(flight, capacity), "expert", split_axis=0, concat_axis=0, tiled=True
     )
@@ -419,9 +477,13 @@
     return (route_grad, pre_grad.reshape(saved_preact.shape), own[None])
 
 
+CHUNKS = (("z", 2048), ("z", 2048))
+ORDER = (0, "gather", 0, 1, 0, 1, 0, 1, 0, 1, "act", 1)
+
+
 def solution(mesh):
     return jax.shard_map(
-        functools.partial(per_device, 2560),
+        functools.partial(per_device, CHUNKS, ORDER),
         mesh=mesh,
         in_specs=(
             P(("dp", "expert"), None),

time: 286 us -> 243 us (0.85)
  waiting for transfers between devices: 151 us -> 107 us
  local copies, waits for them, and re-layouts: 20.1 us -> 11.1 us
  Pallas kernels: 51.8 us -> 59.6 us
    ppermute x12 -> x16, waiting for transfers between devices: 103 us -> 60.5 us  [the longest x8 60.5 us: step(): lax.ppermute(made[1], 'dp', neighbours(axis, 1))]
    all_to_all x2, waiting for transfers between devices: 45.6 us -> 30.1 us  [dispatch(): lax.all_to_all(part.reshape(flight, capacity, width), 'expert', split_axi...]
    all_to_all x2, waiting for transfers between devices: 0.01 us -> 10.2 us  [exchange(): lax.all_to_all(part, 'dp', split_axis=0, concat_axis=0, tiled=True, axis_...]
    unnamed x32 -> x34, local copies, waits for them, and re-layouts: 19.4 us -> 10.4 us
    ppermute x12 -> x16, starting transfers between devices: 17.5 us -> 21.8 us  [the longest x8 18.5 us: step(): lax.ppermute(made[0], 'dp', neighbours(axis, -1))]
    all_gather x1 -> x2, waiting for transfers between devices: 0.01 us -> 4.26 us  [the longest x1 4.26 us: per_device(): lax.all_gather(down_weight[0], 'dp', axis=0, axis_index_groups=ALONG_Z)]
    pallas_call x8 -> x10, Pallas kernels: 28.2 us -> 32.4 us  [call(): pl.pallas_call(kernel, grid_spec=pltpu.PrefetchScalarGridSpec(num_scalar_...]
    pallas_call x2 -> x4, Pallas kernels: 17.4 us -> 19.8 us  [the longest x1 17 us: act_side(): pl.pallas_call(functools.partial(act_kernel, starts, units), grid=(count,...]
  transfers between devices with their start and end apart: 18 -> 23, of which waited for: 11 -> 12; matrix products, arithmetic and copies ran while one was open for 0% -> 0% of each run, Pallas kernels for 18% -> 23%
where the time goes in v2:
time: 243 us; the launch traced here: 242 us
  waiting for transfers between devices  107 us (44%)
  Pallas kernels  59.6 us (25%)
  starting transfers between devices  50.2 us (21%)
  between operations  14.2 us (6%)
  local copies, waits for them, and re-layouts  11.1 us (5%)
    ppermute x8, waiting for transfers between devices, step(): lax.ppermute(made[1], 'dp', neighbours(axis, 1))  60.5 us
    pallas_call x10, Pallas kernels, call(): pl.pallas_call(kernel, grid_spec=pltpu.PrefetchScalarGridSpec(num_scalar_...  32.4 us
    all_to_all x2, waiting for transfers between devices, dispatch(): lax.all_to_all(part.reshape(flight, capacity, width), 'expert', split_axi...  30.1 us
    ppermute x8, starting transfers between devices, step(): lax.ppermute(made[0], 'dp', neighbours(axis, -1))  18.5 us
    pallas_call x1, Pallas kernels, act_side(): pl.pallas_call(functools.partial(act_kernel, starts, units), grid=(count,...  17 us
    all_to_all x2, starting transfers between devices, dispatch(): lax.all_to_all(part.reshape(flight, capacity, width), 'expert', split_axi...  12.8 us
    unnamed x34, local copies, waits for them, and re-layouts  10.4 us
    all_to_all x2, waiting for transfers between devices, exchange(): lax.all_to_all(part, 'dp', split_axis=0, concat_axis=0, tiled=True, axis_...  10.2 us
  transfers between devices with their start and end apart: 23, of which 12 were waited for; matrix products, arithmetic and copies ran while one was open for 0% of the time, Pallas kernels for 23%

profile of v2, /device:TPU:1, one launch (start us, length us, event | category | flops | bytes accessed | tf_op | source)
XLA Modules:
  0.0 241.8 jit_solution(13188164376434120508)
XLA Ops:
  14.4 7.5 %all-to-all-start = ((bf16[8,64,2176]{2,1,0:T(8,128)(2,1)}), bf16[8,64,2176]{2,1,0:T(8,128)(2,1)}, u32[]{:S(2)}, u32[]{:S(2)}) async-start(bf16[8,64,2176]{2,1,0:T(8,128)(2,1)} %bitcast.39), calls=%async_computation | async-start | bytes 4456448 | tf_op jit(solution)/shard_map/all_to_all | solution.py:446
  27.9 21.8 %all-to-all-done = bf16[8,64,2176]{2,1,0:T(8,128)(2,1)} async-done(((bf16[8,64,2176]{2,1,0:T(8,128)(2,1)}), bf16[8,64,2176]{2,1,0:T(8,128)(2,1)}, u32[]{:S(2)}, u32[]{:S(2)}) %all-to-all-start) | async-done | bytes 2228256 | tf_op jit(solution)/shard_map/all_to_all | solution.py:446
  54.1 4.3 %all-gather.4.cloned.1.call-done.array_ref = bf16[8,48,4096]{2,1,0:T(8,128)(2,1)} async-done(((bf16[1,48,4096]{2,1,0:T(8,128)(2,1)}), bf16[8,48,4096]{2,1,0:T(8,128)(2,1)}) %all-gather.4.cloned.1.call-update) | async-done | bytes 3145744 | tf_op jit(solution)/shard_map/all_gather | solution.py:431
  58.4 5.3 %all-to-all-start.1 = ((bf16[8,64,2048]{2,1,0:T(8,128)(2,1)}), bf16[8,64,2048]{2,1,0:T(8,128)(2,1)}, u32[]{:S(2)}, u32[]{:S(2)}) async-start(bf16[8,64,2048]{2,1,0:T(8,128)(2,1)} %bitcast.38), calls=%async_computation.1 | async-start | bytes 4194304 | tf_op jit(solution)/shard_map/all_to_all | solution.py:446
  66.4 9.0 %collective-permute-done.1.got_u = bf16[96,2048]{1,0:T(8,128)(2,1)S(1)} collective-permute-done((bf16[96,2048]{1,0:T(8,128)(2,1)S(1)}, bf16[96,2048]{1,0:T(8,128)(2,1)S(1)}, u32[]{:S(2)}, u32[]{:S(2)}) %collective-permute-start.1) | collective-permute-done | bytes 393248 | tf_op jit(solution)/shard_map/ppermute | solution.py:277
  75.5 3.8 %middle_z.6 = (bf16[192,2048]{1,0:T(8,128)(2,1)S(1)}, bf16[192,2048]{1,0:T(8,128)(2,1)}) custom-call(s32[2]{0:T(128)S(1)} %pad_add_fusion.at_ref, bf16[8,192,512]{2,1,0:T(8,128)(2,1)S(1)} %bitcast.19, bf16[8,192,512]{2,1,0:T(8,128)(2,1)S(1)} %bitcast.20, f32[8,512]{1,0:T(8,128)S(1)} %scale.1.scale_ref.after_ref, ...), custom_call_target="tpu_custom_call" | custom-call | flops 393216 | bytes 192 | tf_op jit(solution)/shard_map/middle_z/pallas_call | solution.py:244
  81.9 8.3 %all-to-all-done.1 = bf16[8,64,2048]{2,1,0:T(8,128)(2,1)} async-done(((bf16[8,64,2048]{2,1,0:T(8,128)(2,1)}), bf16[8,64,2048]{2,1,0:T(8,128)(2,1)}, u32[]{:S(2)}, u32[]{:S(2)}) %all-to-all-start.1) | async-done | bytes 2097184 | tf_op jit(solution)/shard_map/all_to_all | solution.py:446
  98.8 3.2 %middle_z.7 = (bf16[192,2048]{1,0:T(8,128)(2,1)S(1)}, bf16[192,2048]{1,0:T(8,128)(2,1)S(1)}) custom-call(s32[2]{0:T(128)S(1)} %copy-done.9, bf16[8,192,512]{2,1,0:T(8,128)(2,1)S(1)} %bitcast.22, bf16[8,192,512]{2,1,0:T(8,128)(2,1)S(1)} %bitcast.23, f32[8,512]{1,0:T(8,128)S(1)} %scale.1.scale_ref.after_ref, bf16[512,2176]{1,0:T(8,128)(2,1)} %bitcast.3.w_ref.rows_ref.refs_0_, ...), custom_call_target="tpu_custom_call" | custom-call | flops 393216 | bytes 192 | tf_op jit(solution)/shard_map/middle_z/pallas_call | solution.py:244
  107.2 3.1 %middle_z.8 = (bf16[192,2048]{1,0:T(8,128)(2,1)S(1)}, bf16[192,2048]{1,0:T(8,128)(2,1)S(1)}) custom-call(s32[2]{0:T(128)S(1)} %copy-done.10, bf16[8,192,512]{2,1,0:T(8,128)(2,1)S(1)} %bitcast.24, bf16[8,192,512]{2,1,0:T(8,128)(2,1)S(1)} %bitcast.25, f32[8,512]{1,0:T(8,128)S(1)} %scale.1.scale_ref.after_ref, bf16[512,2048]{1,0:T(8,128)(2,1)} %bitcast.9.rows_ref.refs_1_, ...), custom_call_target="tpu_custom_call" | custom-call | flops 393216 | bytes 192 | tf_op jit(solution)/shard_map/middle_z/pallas_call | solution.py:244
  113.1 11.0 %collective-permute-done.9.got_u = bf16[192,2048]{1,0:T(8,128)(2,1)S(1)} collective-permute-done((bf16[192,2048]{1,0:T(8,128)(2,1)S(1)}, bf16[192,2048]{1,0:T(8,128)(2,1)S(1)}, u32[]{:S(2)}, u32[]{:S(2)}) %collective-permute-start.9) | collective-permute-done | bytes 786464 | tf_op jit(solution)/shard_map/ppermute | solution.py:277
  124.0 3.1 %middle_z.9 = (bf16[192,2048]{1,0:T(8,128)(2,1)S(1)}, bf16[192,2048]{1,0:T(8,128)(2,1)S(1)}) custom-call(s32[2]{0:T(128)S(1)} %copy-done.10, bf16[8,192,512]{2,1,0:T(8,128)(2,1)S(1)} %bitcast.26, bf16[8,192,512]{2,1,0:T(8,128)(2,1)S(1)} %bitcast.27, f32[8,512]{1,0:T(8,128)S(1)} %scale.1.scale_ref.after_ref, bf16[512,2176]{1,0:T(8,128)(2,1)} %bitcast.3.w_ref.rows_ref.refs_0_, ...), custom_call_target="tpu_custom_call" | custom-call | flops 393216 | bytes 192 | tf_op jit(solution)/shard_map/middle_z/pallas_call | solution.py:244
  129.9 11.0 %collective-permute-done.7.got_u = bf16[192,2048]{1,0:T(8,128)(2,1)S(1)} collective-permute-done((bf16[192,2048]{1,0:T(8,128)(2,1)S(1)}, bf16[192,2048]{1,0:T(8,128)(2,1)S(1)}, u32[]{:S(2)}, u32[]{:S(2)}) %collective-permute-start.7) | collective-permute-done | bytes 786464 | tf_op jit(solution)/shard_map/ppermute | solution.py:277
  140.9 3.1 %middle_z.10 = (bf16[192,2048]{1,0:T(8,128)(2,1)S(1)}, bf16[192,2048]{1,0:T(8,128)(2,1)S(1)}) custom-call(s32[2]{0:T(128)S(1)} %copy-done.10, bf16[8,192,512]{2,1,0:T(8,128)(2,1)S(1)} %bitcast.28, bf16[8,192,512]{2,1,0:T(8,128)(2,1)S(1)} %bitcast.29, f32[8,512]{1,0:T(8,128)S(1)} %scale.1.scale_ref.after_ref, bf16[512,2048]{1,0:T(8,128)(2,1)} %bitcast.9.rows_ref.refs_1_, ...), custom_call_target="tpu_custom_call" | custom-call | flops 393216 | bytes 192 | tf_op jit(solution)/shard_map/middle_z/pallas_call | solution.py:244
  146.8 11.0 %collective-permute-done.13.got_u = bf16[192,2048]{1,0:T(8,128)(2,1)S(1)} collective-permute-done((bf16[192,2048]{1,0:T(8,128)(2,1)S(1)}, bf16[192,2048]{1,0:T(8,128)(2,1)S(1)}, u32[]{:S(2)}, u32[]{:S(2)}) %collective-permute-start.13) | collective-permute-done | bytes 786464 | tf_op jit(solution)/shard_map/ppermute | solution.py:277
  157.7 3.3 %last_z.2.after_ref = bf16[192,2048]{1,0:T(8,128)(2,1)} custom-call(s32[2]{0:T(128)S(1)} %copy-done.10, bf16[8,192,512]{2,1,0:T(8,128)(2,1)S(1)} %bitcast.30, f32[8,512]{1,0:T(8,128)S(1)} %scale.1.scale_ref.after_ref, bf16[512,2176]{1,0:T(8,128)(2,1)} %bitcast.3.w_ref.rows_ref.refs_0_, bf16[192,2048]{1,0:T(8,128)(2,1)S(1)} %collective-permute-done.12.got_d, ...), custom_call_target="tpu_custom_call" | custom-call | flops 393216 | bytes 192 | tf_op jit(solution)/shard_map/last_z/pallas_call | solution.py:244
  161.1 13.5 %collective-permute-done.11.got_u = bf16[192,2048]{1,0:T(8,128)(2,1)S(1)} collective-permute-done((bf16[192,2048]{1,0:T(8,128)(2,1)S(1)}, bf16[192,2048]{1,0:T(8,128)(2,1)S(1)}, u32[]{:S(2)}, u32[]{:S(2)}) %collective-permute-start.11) | collective-permute-done | bytes 786464 | tf_op jit(solution)/shard_map/ppermute | solution.py:277
  174.6 3.8 %middle_z.11 = (bf16[192,2048]{1,0:T(8,128)(2,1)S(1)}, bf16[192,2048]{1,0:T(8,128)(2,1)}) custom-call(s32[2]{0:T(128)S(1)} %copy-done.10, bf16[8,192,512]{2,1,0:T(8,128)(2,1)S(1)} %bitcast.31, bf16[8,192,512]{2,1,0:T(8,128)(2,1)S(1)} %bitcast.32, f32[8,512]{1,0:T(8,128)S(1)} %scale.1.scale_ref.after_ref, bf16[512,2048]{1,0:T(8,128)(2,1)} %bitcast.9.rows_ref.refs_1_, ...), custom_call_target="tpu_custom_call" | custom-call | flops 393216 | bytes 192 | tf_op jit(solution)/shard_map/middle_z/pallas_call | solution.py:244
  181.0 4.0 %all-to-all-start.3 = ((bf16[4,48,2048]{2,1,0:T(8,128)(2,1)}), bf16[4,48,2048]{2,1,0:T(8,128)(2,1)S(1)}, u32[]{:S(2)}, u32[]{:S(2)}) async-start(bf16[4,48,2048]{2,1,0:T(8,128)(2,1)} %bitcast.15), calls=%async_computation.3 | async-start | bytes 1572864 | tf_op jit(solution)/shard_map/all_to_all | solution.py:286
  186.9 17.0 %act_side.1 = (bf16[512,3072]{1,0:T(8,128)(2,1)}, f32[8,512]{1,0:T(8,128)S(1)}) custom-call(bf16[512,2176]{1,0:T(8,128)(2,1)} %bitcast.3.w_ref.rows_ref.refs_0_, bf16[512,2048]{1,0:T(8,128)(2,1)} %bitcast.9.rows_ref.refs_1_, bf16[4,8,48,4096]{3,2,1,0:T(8,128)(2,1)} %bitcast.44, bf16[512,3072]{1,0:T(8,128)(2,1)S(1)} %bitcast.36, ...), custom_call_target="tpu_custom_call" | custom-call | flops 6442450944 | bytes 23068672 | tf_op jit(solution)/shard_map/act_side/pallas_call | solution.py:373
  204.6 7.1 %all-to-all-start.2 = ((f32[8,1,64]{2,1,0:T(1,128)}), f32[8,1,64]{2,1,0:T(1,128)S(1)}, u32[]{:S(2)}, u32[]{:S(2)}) async-start(f32[8,1,64]{2,1,0:T(1,128)} %bitcast.11), calls=%async_computation.2 | async-start | bytes 8192 | tf_op jit(solution)/shard_map/all_to_all | solution.py:473
  211.7 3.7 %last_z.3 = bf16[192,2048]{1,0:T(8,128)(2,1)} custom-call(s32[2]{0:T(128)S(1)} %copy-done.11, bf16[8,192,512]{2,1,0:T(8,128)(2,1)S(1)} %bitcast.33, f32[8,512]{1,0:T(8,128)S(1)} %scale.1.scale_ref.after_ref, bf16[512,2048]{1,0:T(8,128)(2,1)} %bitcast.9.rows_ref.refs_1_, bf16[192,2048]{1,0:T(8,128)(2,1)} %collective-permute-done.14.got_d, ...), custom_call_target="tpu_custom_call" | custom-call | flops 393216 | bytes 192 | tf_op jit(solution)/shard_map/last_z/pallas_call | solution.py:244
  216.2 4.5 %all-to-all-start.4 = ((bf16[4,48,2048]{2,1,0:T(8,128)(2,1)}), bf16[4,48,2048]{2,1,0:T(8,128)(2,1)S(1)}, u32[]{:S(2)}, u32[]{:S(2)}) async-start(bf16[4,48,2048]{2,1,0:T(8,128)(2,1)} %bitcast.16), calls=%async_computation.4 | async-start | bytes 1572864 | tf_op jit(solution)/shard_map/all_to_all | solution.py:286
  221.9 10.2 %all-to-all-done.4.refs_1_ = bf16[4,48,2048]{2,1,0:T(8,128)(2,1)S(1)} async-done(((bf16[4,48,2048]{2,1,0:T(8,128)(2,1)}), bf16[4,48,2048]{2,1,0:T(8,128)(2,1)S(1)}, u32[]{:S(2)}, u32[]{:S(2)}) %all-to-all-start.4) | async-done | bytes 786464 | tf_op jit(solution)/shard_map/all_to_all | solution.py:286
  232.1 2.9 %sum_parts.1 = f32[48,4096]{1,0:T(8,128)} custom-call(bf16[4,48,2048]{2,1,0:T(8,128)(2,1)S(1)} %all-to-all-done.3.refs_0_, bf16[4,48,2048]{2,1,0:T(8,128)(2,1)S(1)} %all-to-all-done.4.refs_1_), custom_call_target="tpu_custom_call" | custom-call | flops 786432 | bytes 2359296 | tf_op jit(solution)/shard_map/sum_parts/pallas_call | solution.py:311
  (80 shorter events, 52.2 us)
Async XLA Ops:
  7.2 51.2 %all-gather.4.cloned.1.call-start = ((), (), s32[]{:S(2)}) async-start(), calls=%async_computation.5 | async-start | bytes 3538944 | tf_op jit(solution)/shard_map/all_gather | solution.py:431
  14.4 35.3 %all-to-all-start = ((bf16[8,64,2176]{2,1,0:T(8,128)(2,1)}), bf16[8,64,2176]{2,1,0:T(8,128)(2,1)}, u32[]{:S(2)}, u32[]{:S(2)}) async-start(bf16[8,64,2176]{2,1,0:T(8,128)(2,1)} %bitcast.39), calls=%async_computation | async-start | bytes 4456448 | tf_op jit(solution)/shard_map/all_to_all | solution.py:446
  21.9 163.1 %all-gather.6.cloned.1.call-start = ((), (), s32[]{:S(2)}) async-start(), calls=%async_computation.6 | async-start | bytes 15728640 | tf_op jit(solution)/shard_map/all_gather | solution.py:456
  27.9 47.5 %copy-start.8 = (s32[2]{0:T(128)}, s32[2]{0:T(128)S(1)}, u32[]{:S(2)}) copy-start(s32[2]{0:T(128)S(1)} %pad_add_fusion.at_ref) | copy-start | bytes 28
  58.4 31.8 %all-to-all-start.1 = ((bf16[8,64,2048]{2,1,0:T(8,128)(2,1)}), bf16[8,64,2048]{2,1,0:T(8,128)(2,1)}, u32[]{:S(2)}, u32[]{:S(2)}) async-start(bf16[8,64,2048]{2,1,0:T(8,128)(2,1)} %bitcast.38), calls=%async_computation.1 | async-start | bytes 4194304 | tf_op jit(solution)/shard_map/all_to_all | solution.py:446
  63.7 11.7 %collective-permute-start.1 = (bf16[96,2048]{1,0:T(8,128)(2,1)S(1)}, bf16[96,2048]{1,0:T(8,128)(2,1)S(1)}, u32[]{:S(2)}, u32[]{:S(2)}) collective-permute-start(bf16[96,2048]{1,0:T(8,128)(2,1)S(1)} %get-tuple-element.27), channel_id=1, source_target_pairs={{0,32},{8,40},{16,48},{24,56},{32,64},{40,72},{48,80},{56,88},{64,... | collective-permute-start | bytes 1179656 | tf_op jit(solution)/shard_map/ppermute | solution.py:277
  64.7 10.8 %collective-permute-start = (bf16[96,2048]{1,0:T(8,128)(2,1)S(1)}, bf16[96,2048]{1,0:T(8,128)(2,1)S(1)}, u32[]{:S(2)}, u32[]{:S(2)}) collective-permute-start(bf16[96,2048]{1,0:T(8,128)(2,1)S(1)} %copy-done.6), channel_id=1, source_target_pairs={{0,224},{8,232},{16,240},{24,248},{32,0},{40,8},{48,16},{56,24},{6... | collective-permute-start | bytes 1179656 | tf_op jit(solution)/shard_map/ppermute | solution.py:276
  79.2 19.5 %collective-permute-start.5 = (bf16[192,2048]{1,0:T(8,128)(2,1)}, bf16[192,2048]{1,0:T(8,128)(2,1)S(1)}, u32[]{:S(2)}, u32[]{:S(2)}) collective-permute-start(bf16[192,2048]{1,0:T(8,128)(2,1)} %get-tuple-element.31), channel_id=1, source_target_pairs={{0,32},{8,40},{16,48},{24,56},{32,64},{40,72},{48,80},{56,88},{64,... | collective-permute-start | bytes 2359304 | tf_op jit(solution)/shard_map/ppermute | solution.py:277
  79.9 18.9 %collective-permute-start.4 = (bf16[192,2048]{1,0:T(8,128)(2,1)S(1)}, bf16[192,2048]{1,0:T(8,128)(2,1)}, u32[]{:S(2)}, u32[]{:S(2)}) collective-permute-start(bf16[192,2048]{1,0:T(8,128)(2,1)S(1)} %get-tuple-element.28.after_ref), channel_id=1, source_target_pairs={{0,224},{8,232},{16,240},{24,248},{32,0},{40,8},{48,16},{56,24},{6... | collective-permute-start | bytes 2359304 | tf_op jit(solution)/shard_map/ppermute | solution.py:276
  93.4 13.7 %collective-permute-start.3 = (bf16[96,2048]{1,0:T(8,128)(2,1)S(1)}, bf16[96,2048]{1,0:T(8,128)(2,1)S(1)}, u32[]{:S(2)}, u32[]{:S(2)}) collective-permute-start(bf16[96,2048]{1,0:T(8,128)(2,1)S(1)} %get-tuple-element.30), channel_id=1, source_target_pairs={{0,32},{8,40},{16,48},{24,56},{32,64},{40,72},{48,80},{56,88},{64,... | collective-permute-start | bytes 1179656 | tf_op jit(solution)/shard_map/ppermute | solution.py:277
  94.5 12.7 %collective-permute-start.2 = (bf16[96,2048]{1,0:T(8,128)(2,1)S(1)}, bf16[96,2048]{1,0:T(8,128)(2,1)S(1)}, u32[]{:S(2)}, u32[]{:S(2)}) collective-permute-start(bf16[96,2048]{1,0:T(8,128)(2,1)S(1)} %get-tuple-element.29.after_ref), channel_id=1, source_target_pairs={{0,224},{8,232},{16,240},{24,248},{32,0},{40,8},{48,16},{56,24},{6... | collective-permute-start | bytes 1179656 | tf_op jit(solution)/shard_map/ppermute | solution.py:276
  102.0 22.1 %collective-permute-start.9 = (bf16[192,2048]{1,0:T(8,128)(2,1)S(1)}, bf16[192,2048]{1,0:T(8,128)(2,1)S(1)}, u32[]{:S(2)}, u32[]{:S(2)}) collective-permute-start(bf16[192,2048]{1,0:T(8,128)(2,1)S(1)} %get-tuple-element.35), channel_id=1, source_target_pairs={{0,32},{8,40},{16,48},{24,56},{32,64},{40,72},{48,80},{56,88},{64,... | collective-permute-start | bytes 2359304 | tf_op jit(solution)/shard_map/ppermute | solution.py:277
  102.3 21.8 %collective-permute-start.8 = (bf16[192,2048]{1,0:T(8,128)(2,1)S(1)}, bf16[192,2048]{1,0:T(8,128)(2,1)S(1)}, u32[]{:S(2)}, u32[]{:S(2)}) collective-permute-start(bf16[192,2048]{1,0:T(8,128)(2,1)S(1)} %get-tuple-element.32.after_ref), channel_id=1, source_target_pairs={{0,224},{8,232},{16,240},{24,248},{32,0},{40,8},{48,16},{56,24},{6... | collective-permute-start | bytes 2359304 | tf_op jit(solution)/shard_map/ppermute | solution.py:276
  110.3 30.6 %collective-permute-start.7 = (bf16[192,2048]{1,0:T(8,128)(2,1)S(1)}, bf16[192,2048]{1,0:T(8,128)(2,1)S(1)}, u32[]{:S(2)}, u32[]{:S(2)}) collective-permute-start(bf16[192,2048]{1,0:T(8,128)(2,1)S(1)} %get-tuple-element.34), channel_id=1, source_target_pairs={{0,32},{8,40},{16,48},{24,56},{32,64},{40,72},{48,80},{56,88},{64,... | collective-permute-start | bytes 2359304 | tf_op jit(solution)/shard_map/ppermute | solution.py:277
  110.6 30.3 %collective-permute-start.6 = (bf16[192,2048]{1,0:T(8,128)(2,1)S(1)}, bf16[192,2048]{1,0:T(8,128)(2,1)S(1)}, u32[]{:S(2)}, u32[]{:S(2)}) collective-permute-start(bf16[192,2048]{1,0:T(8,128)(2,1)S(1)} %get-tuple-element.33.after_ref), channel_id=1, source_target_pairs={{0,224},{8,232},{16,240},{24,248},{32,0},{40,8},{48,16},{56,24},{6... | collective-permute-start | bytes 2359304 | tf_op jit(solution)/shard_map/ppermute | solution.py:276
  127.2 30.6 %collective-permute-start.13 = (bf16[192,2048]{1,0:T(8,128)(2,1)S(1)}, bf16[192,2048]{1,0:T(8,128)(2,1)S(1)}, u32[]{:S(2)}, u32[]{:S(2)}) collective-permute-start(bf16[192,2048]{1,0:T(8,128)(2,1)S(1)} %get-tuple-element.39), channel_id=1, source_target_pairs={{0,32},{8,40},{16,48},{24,56},{32,64},{40,72},{48,80},{56,88},{64,... | collective-permute-start | bytes 2359304 | tf_op jit(solution)/shard_map/ppermute | solution.py:277
  127.3 30.5 %collective-permute-start.12 = (bf16[192,2048]{1,0:T(8,128)(2,1)S(1)}, bf16[192,2048]{1,0:T(8,128)(2,1)S(1)}, u32[]{:S(2)}, u32[]{:S(2)}) collective-permute-start(bf16[192,2048]{1,0:T(8,128)(2,1)S(1)} %get-tuple-element.36.after_ref), channel_id=1, source_target_pairs={{0,224},{8,232},{16,240},{24,248},{32,0},{40,8},{48,16},{56,24},{6... | collective-permute-start | bytes 2359304 | tf_op jit(solution)/shard_map/ppermute | solution.py:276
  144.0 30.6 %collective-permute-start.11 = (bf16[192,2048]{1,0:T(8,128)(2,1)S(1)}, bf16[192,2048]{1,0:T(8,128)(2,1)S(1)}, u32[]{:S(2)}, u32[]{:S(2)}) collective-permute-start(bf16[192,2048]{1,0:T(8,128)(2,1)S(1)} %get-tuple-element.38), channel_id=1, source_target_pairs={{0,32},{8,40},{16,48},{24,56},{32,64},{40,72},{48,80},{56,88},{64,... | collective-permute-start | bytes 2359304 | tf_op jit(solution)/shard_map/ppermute | solution.py:277
  144.1 30.5 %collective-permute-start.10 = (bf16[192,2048]{1,0:T(8,128)(2,1)S(1)}, bf16[192,2048]{1,0:T(8,128)(2,1)S(1)}, u32[]{:S(2)}, u32[]{:S(2)}) collective-permute-start(bf16[192,2048]{1,0:T(8,128)(2,1)S(1)} %get-tuple-element.37.after_ref), channel_id=1, source_target_pairs={{0,224},{8,232},{16,240},{24,248},{32,0},{40,8},{48,16},{56,24},{6... | collective-permute-start | bytes 2359304 | tf_op jit(solution)/shard_map/ppermute | solution.py:276
  178.4 33.3 %collective-permute-start.15 = (bf16[192,2048]{1,0:T(8,128)(2,1)}, bf16[192,2048]{1,0:T(8,128)(2,1)}, u32[]{:S(2)}, u32[]{:S(2)}) collective-permute-start(bf16[192,2048]{1,0:T(8,128)(2,1)} %get-tuple-element.44), channel_id=1, source_target_pairs={{0,32},{8,40},{16,48},{24,56},{32,64},{40,72},{48,80},{56,88},{64,... | collective-permute-start | bytes 2359304 | tf_op jit(solution)/shard_map/ppermute | solution.py:277
  178.4 33.3 %collective-permute-start.14 = (bf16[192,2048]{1,0:T(8,128)(2,1)S(1)}, bf16[192,2048]{1,0:T(8,128)(2,1)}, u32[]{:S(2)}, u32[]{:S(2)}) collective-permute-start(bf16[192,2048]{1,0:T(8,128)(2,1)S(1)} %get-tuple-element.40.refs_5_), channel_id=1, source_target_pairs={{0,224},{8,232},{16,240},{24,248},{32,0},{40,8},{48,16},{56,24},{6... | collective-permute-start | bytes 2359304 | tf_op jit(solution)/shard_map/ppermute | solution.py:276
  181.0 23.5 %all-to-all-start.3 = ((bf16[4,48,2048]{2,1,0:T(8,128)(2,1)}), bf16[4,48,2048]{2,1,0:T(8,128)(2,1)S(1)}, u32[]{:S(2)}, u32[]{:S(2)}) async-start(bf16[4,48,2048]{2,1,0:T(8,128)(2,1)} %bitcast.15), calls=%async_computation.3 | async-start | bytes 1572864 | tf_op jit(solution)/shard_map/all_to_all | solution.py:286
  204.6 11.6 %all-to-all-start.2 = ((f32[8,1,64]{2,1,0:T(1,128)}), f32[8,1,64]{2,1,0:T(1,128)S(1)}, u32[]{:S(2)}, u32[]{:S(2)}) async-start(f32[8,1,64]{2,1,0:T(1,128)} %bitcast.11), calls=%async_computation.2 | async-start | bytes 8192 | tf_op jit(solution)/shard_map/all_to_all | solution.py:473
  216.2 15.9 %all-to-all-start.4 = ((bf16[4,48,2048]{2,1,0:T(8,128)(2,1)}), bf16[4,48,2048]{2,1,0:T(8,128)(2,1)S(1)}, u32[]{:S(2)}, u32[]{:S(2)}) async-start(bf16[4,48,2048]{2,1,0:T(8,128)(2,1)} %bitcast.16), calls=%async_computation.4 | async-start | bytes 1572864 | tf_op jit(solution)/shard_map/all_to_all | solution.py:286
  (16 other events, 87.9 us)
Sparse Core Ops, SparseCore 0:
  9.8 48.5 all-gather.3
  60.2 120.0 all-gather.5

commit v3 on v2

--- a/solution.py
+++ b/solution.py
@@ -470,9 +470,8 @@
         if arrived[item] is None:
             parts[item] = exchange(made, "y" if axis == "z" else "z")
     own = sum_parts([parts[k] for k in range(len(chunks))])
-    back = lax.all_to_all(
-        route[0].reshape(flight, capacity), "expert", split_axis=0, concat_axis=0, tiled=True
-    )
+    every = lax.all_gather(route[0], "expert").reshape(flight, flight, capacity)
+    back = lax.dynamic_index_in_dim(every, lax.axis_index("expert"), 1, keepdims=False)
     route_grad = combine(back, ids_t, rank).T
     return (route_grad, pre_grad.reshape(saved_preact.shape), own[None])
 

time: 243 us -> 239 us (0.984)
  blocking collectives: 0 us -> 15 us
  waiting for transfers between devices: 107 us -> 95.6 us
  starting transfers between devices: 50.2 us -> 42.8 us
    all_gather x0 -> x1, blocking collectives: none -> 15 us  [per_device(): every = lax.all_gather(route[0], 'expert').reshape(flight, flight, capacity)]
    all_to_all x2, waiting for transfers between devices: 10.2 us -> 0.01 us  [exchange(): lax.all_to_all(part, 'dp', split_axis=0, concat_axis=0, tiled=True, axis_...]
    all_to_all x1 -> x0, starting transfers between devices: 7.07 us -> none  [per_device(): lax.all_to_all(route[0].reshape(flight, capacity), 'expert', split_axis=0...]
    unnamed x34 -> x35, local copies, waits for them, and re-layouts: 10.4 us -> 10.5 us
  transfers between devices with their start and end apart: 23 -> 22, of which waited for: 12 -> 10; matrix products, arithmetic and copies ran while one was open for 0% -> 0% of each run, Pallas kernels for 23% -> 24%
where the time goes in v3:
time: 239 us; the launch traced here: 238 us
  waiting for transfers between devices  95.6 us (40%)
  Pallas kernels  59.6 us (25%)
  starting transfers between devices  42.8 us (18%)
  blocking collectives  15 us (6%)
  between operations  14.3 us (6%)
  local copies, waits for them, and re-layouts  10.6 us (4%)
    ppermute x8, waiting for transfers between devices, step(): lax.ppermute(made[1], 'dp', neighbours(axis, 1))  60.5 us
    pallas_call x10, Pallas kernels, call(): pl.pallas_call(kernel, grid_spec=pltpu.PrefetchScalarGridSpec(num_scalar_...  32.4 us
    all_to_all x2, waiting for transfers between devices, dispatch(): lax.all_to_all(part.reshape(flight, capacity, width), 'expert', split_axi...  30 us
    ppermute x8, starting transfers between devices, step(): lax.ppermute(made[0], 'dp', neighbours(axis, -1))  18.5 us
    pallas_call x1, Pallas kernels, act_side(): pl.pallas_call(functools.partial(act_kernel, starts, units), grid=(count,...  17 us
    all_gather x1, blocking collectives, per_device(): every = lax.all_gather(route[0], 'expert').reshape(flight, flight, capacity)  15 us
    all_to_all x2, starting transfers between devices, dispatch(): lax.all_to_all(part.reshape(flight, capacity, width), 'expert', split_axi...  12.8 us
    unnamed x35, local copies, waits for them, and re-layouts  10.5 us
  transfers between devices with their start and end apart: 22, of which 10 were waited for; matrix products, arithmetic and copies ran while one was open for 0% of the time, Pallas kernels for 24%

profile of v3, /device:TPU:1, one launch (start us, length us, event | category | flops | bytes accessed | tf_op | source)
XLA Modules:
  0.0 238.0 jit_solution(1540293117406102642)
XLA Ops:
  14.4 7.5 %all-to-all-start = ((bf16[8,64,2176]{2,1,0:T(8,128)(2,1)}), bf16[8,64,2176]{2,1,0:T(8,128)(2,1)}, u32[]{:S(2)}, u32[]{:S(2)}) async-start(bf16[8,64,2176]{2,1,0:T(8,128)(2,1)} %bitcast.40), calls=%async_computation | async-start | bytes 4456448 | tf_op jit(solution)/shard_map/all_to_all | solution.py:446
  28.0 21.8 %all-to-all-done = bf16[8,64,2176]{2,1,0:T(8,128)(2,1)} async-done(((bf16[8,64,2176]{2,1,0:T(8,128)(2,1)}), bf16[8,64,2176]{2,1,0:T(8,128)(2,1)}, u32[]{:S(2)}, u32[]{:S(2)}) %all-to-all-start) | async-done | bytes 2228256 | tf_op jit(solution)/shard_map/all_to_all | solution.py:446
  54.1 4.3 %all-gather.5.cloned.1.call-done.array_ref = bf16[8,48,4096]{2,1,0:T(8,128)(2,1)} async-done(((bf16[1,48,4096]{2,1,0:T(8,128)(2,1)}), bf16[8,48,4096]{2,1,0:T(8,128)(2,1)}) %all-gather.5.cloned.1.call-update) | async-done | bytes 3145744 | tf_op jit(solution)/shard_map/all_gather | solution.py:431
  58.4 5.3 %all-to-all-start.1 = ((bf16[8,64,2048]{2,1,0:T(8,128)(2,1)}), bf16[8,64,2048]{2,1,0:T(8,128)(2,1)}, u32[]{:S(2)}, u32[]{:S(2)}) async-start(bf16[8,64,2048]{2,1,0:T(8,128)(2,1)} %bitcast.39), calls=%async_computation.1 | async-start | bytes 4194304 | tf_op jit(solution)/shard_map/all_to_all | solution.py:446
  66.4 9.1 %collective-permute-done.1.got_u = bf16[96,2048]{1,0:T(8,128)(2,1)S(1)} collective-permute-done((bf16[96,2048]{1,0:T(8,128)(2,1)S(1)}, bf16[96,2048]{1,0:T(8,128)(2,1)S(1)}, u32[]{:S(2)}, u32[]{:S(2)}) %collective-permute-start.1) | collective-permute-done | bytes 393248 | tf_op jit(solution)/shard_map/ppermute | solution.py:277
  75.5 3.8 %middle_z.6 = (bf16[192,2048]{1,0:T(8,128)(2,1)S(1)}, bf16[192,2048]{1,0:T(8,128)(2,1)}) custom-call(s32[2]{0:T(128)S(1)} %pad_add_fusion.at_ref, bf16[8,192,512]{2,1,0:T(8,128)(2,1)S(1)} %bitcast.20, bf16[8,192,512]{2,1,0:T(8,128)(2,1)S(1)} %bitcast.21, f32[8,512]{1,0:T(8,128)S(1)} %scale.1.scale_ref.after_ref, ...), custom_call_target="tpu_custom_call" | custom-call | flops 393216 | bytes 192 | tf_op jit(solution)/shard_map/middle_z/pallas_call | solution.py:244
  81.9 8.2 %all-to-all-done.1 = bf16[8,64,2048]{2,1,0:T(8,128)(2,1)} async-done(((bf16[8,64,2048]{2,1,0:T(8,128)(2,1)}), bf16[8,64,2048]{2,1,0:T(8,128)(2,1)}, u32[]{:S(2)}, u32[]{:S(2)}) %all-to-all-start.1) | async-done | bytes 2097184 | tf_op jit(solution)/shard_map/all_to_all | solution.py:446
  98.8 3.2 %middle_z.7 = (bf16[192,2048]{1,0:T(8,128)(2,1)S(1)}, bf16[192,2048]{1,0:T(8,128)(2,1)S(1)}) custom-call(s32[2]{0:T(128)S(1)} %copy-done.9, bf16[8,192,512]{2,1,0:T(8,128)(2,1)S(1)} %bitcast.23, bf16[8,192,512]{2,1,0:T(8,128)(2,1)S(1)} %bitcast.24, f32[8,512]{1,0:T(8,128)S(1)} %scale.1.scale_ref.after_ref, bf16[512,2176]{1,0:T(8,128)(2,1)} %bitcast.3.w_ref.rows_ref.refs_0_, ...), custom_call_target="tpu_custom_call" | custom-call | flops 393216 | bytes 192 | tf_op jit(solution)/shard_map/middle_z/pallas_call | solution.py:244
  107.2 3.1 %middle_z.8 = (bf16[192,2048]{1,0:T(8,128)(2,1)S(1)}, bf16[192,2048]{1,0:T(8,128)(2,1)S(1)}) custom-call(s32[2]{0:T(128)S(1)} %copy-done.10, bf16[8,192,512]{2,1,0:T(8,128)(2,1)S(1)} %bitcast.25, bf16[8,192,512]{2,1,0:T(8,128)(2,1)S(1)} %bitcast.26, f32[8,512]{1,0:T(8,128)S(1)} %scale.1.scale_ref.after_ref, bf16[512,2048]{1,0:T(8,128)(2,1)} %bitcast.9.rows_ref.refs_1_, ...), custom_call_target="tpu_custom_call" | custom-call | flops 393216 | bytes 192 | tf_op jit(solution)/shard_map/middle_z/pallas_call | solution.py:244
  113.1 11.0 %collective-permute-done.9.got_u = bf16[192,2048]{1,0:T(8,128)(2,1)S(1)} collective-permute-done((bf16[192,2048]{1,0:T(8,128)(2,1)S(1)}, bf16[192,2048]{1,0:T(8,128)(2,1)S(1)}, u32[]{:S(2)}, u32[]{:S(2)}) %collective-permute-start.9) | collective-permute-done | bytes 786464 | tf_op jit(solution)/shard_map/ppermute | solution.py:277
  124.1 3.1 %middle_z.9 = (bf16[192,2048]{1,0:T(8,128)(2,1)S(1)}, bf16[192,2048]{1,0:T(8,128)(2,1)S(1)}) custom-call(s32[2]{0:T(128)S(1)} %copy-done.10, bf16[8,192,512]{2,1,0:T(8,128)(2,1)S(1)} %bitcast.27, bf16[8,192,512]{2,1,0:T(8,128)(2,1)S(1)} %bitcast.28, f32[8,512]{1,0:T(8,128)S(1)} %scale.1.scale_ref.after_ref, bf16[512,2176]{1,0:T(8,128)(2,1)} %bitcast.3.w_ref.rows_ref.refs_0_, ...), custom_call_target="tpu_custom_call" | custom-call | flops 393216 | bytes 192 | tf_op jit(solution)/shard_map/middle_z/pallas_call | solution.py:244
  130.0 11.0 %collective-permute-done.7.got_u = bf16[192,2048]{1,0:T(8,128)(2,1)S(1)} collective-permute-done((bf16[192,2048]{1,0:T(8,128)(2,1)S(1)}, bf16[192,2048]{1,0:T(8,128)(2,1)S(1)}, u32[]{:S(2)}, u32[]{:S(2)}) %collective-permute-start.7) | collective-permute-done | bytes 786464 | tf_op jit(solution)/shard_map/ppermute | solution.py:277
  140.9 3.1 %middle_z.10 = (bf16[192,2048]{1,0:T(8,128)(2,1)S(1)}, bf16[192,2048]{1,0:T(8,128)(2,1)S(1)}) custom-call(s32[2]{0:T(128)S(1)} %copy-done.10, bf16[8,192,512]{2,1,0:T(8,128)(2,1)S(1)} %bitcast.29, bf16[8,192,512]{2,1,0:T(8,128)(2,1)S(1)} %bitcast.30, f32[8,512]{1,0:T(8,128)S(1)} %scale.1.scale_ref.after_ref, bf16[512,2048]{1,0:T(8,128)(2,1)} %bitcast.9.rows_ref.refs_1_, ...), custom_call_target="tpu_custom_call" | custom-call | flops 393216 | bytes 192 | tf_op jit(solution)/shard_map/middle_z/pallas_call | solution.py:244
  146.8 11.0 %collective-permute-done.13.got_u = bf16[192,2048]{1,0:T(8,128)(2,1)S(1)} collective-permute-done((bf16[192,2048]{1,0:T(8,128)(2,1)S(1)}, bf16[192,2048]{1,0:T(8,128)(2,1)S(1)}, u32[]{:S(2)}, u32[]{:S(2)}) %collective-permute-start.13) | collective-permute-done | bytes 786464 | tf_op jit(solution)/shard_map/ppermute | solution.py:277
  157.8 3.3 %last_z.2.after_ref = bf16[192,2048]{1,0:T(8,128)(2,1)} custom-call(s32[2]{0:T(128)S(1)} %copy-done.10, bf16[8,192,512]{2,1,0:T(8,128)(2,1)S(1)} %bitcast.31, f32[8,512]{1,0:T(8,128)S(1)} %scale.1.scale_ref.after_ref, bf16[512,2176]{1,0:T(8,128)(2,1)} %bitcast.3.w_ref.rows_ref.refs_0_, bf16[192,2048]{1,0:T(8,128)(2,1)S(1)} %collective-permute-done.12.got_d, ...), custom_call_target="tpu_custom_call" | custom-call | flops 393216 | bytes 192 | tf_op jit(solution)/shard_map/last_z/pallas_call | solution.py:244
  161.1 13.5 %collective-permute-done.11.got_u = bf16[192,2048]{1,0:T(8,128)(2,1)S(1)} collective-permute-done((bf16[192,2048]{1,0:T(8,128)(2,1)S(1)}, bf16[192,2048]{1,0:T(8,128)(2,1)S(1)}, u32[]{:S(2)}, u32[]{:S(2)}) %collective-permute-start.11) | collective-permute-done | bytes 786464 | tf_op jit(solution)/shard_map/ppermute | solution.py:277
  174.6 3.8 %middle_z.11 = (bf16[192,2048]{1,0:T(8,128)(2,1)S(1)}, bf16[192,2048]{1,0:T(8,128)(2,1)}) custom-call(s32[2]{0:T(128)S(1)} %copy-done.10, bf16[8,192,512]{2,1,0:T(8,128)(2,1)S(1)} %bitcast.32, bf16[8,192,512]{2,1,0:T(8,128)(2,1)S(1)} %bitcast.33, f32[8,512]{1,0:T(8,128)S(1)} %scale.1.scale_ref.after_ref, bf16[512,2048]{1,0:T(8,128)(2,1)} %bitcast.9.rows_ref.refs_1_, ...), custom_call_target="tpu_custom_call" | custom-call | flops 393216 | bytes 192 | tf_op jit(solution)/shard_map/middle_z/pallas_call | solution.py:244
  178.4 2.7 %collective-permute-start.14 = (bf16[192,2048]{1,0:T(8,128)(2,1)S(1)}, bf16[192,2048]{1,0:T(8,128)(2,1)}, u32[]{:S(2)}, u32[]{:S(2)}) collective-permute-start(bf16[192,2048]{1,0:T(8,128)(2,1)S(1)} %get-tuple-element.40.refs_5_), channel_id=1, source_target_pairs={{0,224},{8,232},{16,240},{24,248},{32,0},{40,8},{48,16},{56,24},{6... | collective-permute-start | bytes 2359304 | tf_op jit(solution)/shard_map/ppermute | solution.py:276
  181.1 4.0 %all-to-all-start.2 = ((bf16[4,48,2048]{2,1,0:T(8,128)(2,1)}), bf16[4,48,2048]{2,1,0:T(8,128)(2,1)S(1)}, u32[]{:S(2)}, u32[]{:S(2)}) async-start(bf16[4,48,2048]{2,1,0:T(8,128)(2,1)} %bitcast.15), calls=%async_computation.2 | async-start | bytes 1572864 | tf_op jit(solution)/shard_map/all_to_all | solution.py:286
  186.9 17.0 %act_side.1 = (bf16[512,3072]{1,0:T(8,128)(2,1)}, f32[8,512]{1,0:T(8,128)S(1)}) custom-call(bf16[512,2176]{1,0:T(8,128)(2,1)} %bitcast.3.w_ref.rows_ref.refs_0_, bf16[512,2048]{1,0:T(8,128)(2,1)} %bitcast.9.rows_ref.refs_1_, bf16[4,8,48,4096]{3,2,1,0:T(8,128)(2,1)} %bitcast.45, bf16[512,3072]{1,0:T(8,128)(2,1)S(1)} %bitcast.37, ...), custom_call_target="tpu_custom_call" | custom-call | flops 6442450944 | bytes 23068672 | tf_op jit(solution)/shard_map/act_side/pallas_call | solution.py:373
  204.0 3.7 %last_z.3 = bf16[192,2048]{1,0:T(8,128)(2,1)} custom-call(s32[2]{0:T(128)S(1)} %copy-done.11, bf16[8,192,512]{2,1,0:T(8,128)(2,1)S(1)} %bitcast.34, f32[8,512]{1,0:T(8,128)S(1)} %scale.1.scale_ref.after_ref, bf16[512,2048]{1,0:T(8,128)(2,1)} %bitcast.9.rows_ref.refs_1_, bf16[192,2048]{1,0:T(8,128)(2,1)} %collective-permute-done.14.got_d, ...), custom_call_target="tpu_custom_call" | custom-call | flops 393216 | bytes 192 | tf_op jit(solution)/shard_map/last_z/pallas_call | solution.py:244
  207.7 4.2 %all-to-all-start.3 = ((bf16[4,48,2048]{2,1,0:T(8,128)(2,1)}), bf16[4,48,2048]{2,1,0:T(8,128)(2,1)S(1)}, u32[]{:S(2)}, u32[]{:S(2)}) async-start(bf16[4,48,2048]{2,1,0:T(8,128)(2,1)} %bitcast.16), calls=%async_computation.3 | async-start | bytes 1572864 | tf_op jit(solution)/shard_map/all_to_all | solution.py:286
  211.9 15.0 %all-gather.1 = f32[8,1,512]{2,1,0:T(1,128)S(1)} all-gather(f32[1,1,512]{2,1,0:T(1,128)S(1)} %slice_bitcast_fusion), channel_id=1, replica_groups=mesh['dp'=32,'expert'=8] {'expert'}, dimensions={0}, use_global_device_ids=true | all-gather | bytes 18432 | tf_op jit(solution)/shard_map/all_gather | solution.py:473
  228.3 2.9 %sum_parts.1 = f32[48,4096]{1,0:T(8,128)} custom-call(bf16[4,48,2048]{2,1,0:T(8,128)(2,1)S(1)} %all-to-all-done.2.refs_0_, bf16[4,48,2048]{2,1,0:T(8,128)(2,1)S(1)} %all-to-all-done.3.refs_1_), custom_call_target="tpu_custom_call" | custom-call | flops 786432 | bytes 2359296 | tf_op jit(solution)/shard_map/sum_parts/pallas_call | solution.py:311
  (81 shorter events, 48.2 us)
Async XLA Ops:
  7.2 51.2 %all-gather.5.cloned.1.call-start = ((), (), s32[]{:S(2)}) async-start(), calls=%async_computation.4 | async-start | bytes 3538944 | tf_op jit(solution)/shard_map/all_gather | solution.py:431
  14.4 35.4 %all-to-all-start = ((bf16[8,64,2176]{2,1,0:T(8,128)(2,1)}), bf16[8,64,2176]{2,1,0:T(8,128)(2,1)}, u32[]{:S(2)}, u32[]{:S(2)}) async-start(bf16[8,64,2176]{2,1,0:T(8,128)(2,1)} %bitcast.40), calls=%async_computation | async-start | bytes 4456448 | tf_op jit(solution)/shard_map/all_to_all | solution.py:446
  21.9 163.2 %all-gather.7.cloned.1.call-start = ((), (), s32[]{:S(2)}) async-start(), calls=%async_computation.5 | async-start | bytes 15728640 | tf_op jit(solution)/shard_map/all_gather | solution.py:456
  28.0 47.5 %copy-start.8 = (s32[2]{0:T(128)}, s32[2]{0:T(128)S(1)}, u32[]{:S(2)}) copy-start(s32[2]{0:T(128)S(1)} %pad_add_fusion.at_ref) | copy-start | bytes 28
  58.4 31.8 %all-to-all-start.1 = ((bf16[8,64,2048]{2,1,0:T(8,128)(2,1)}), bf16[8,64,2048]{2,1,0:T(8,128)(2,1)}, u32[]{:S(2)}, u32[]{:S(2)}) async-start(bf16[8,64,2048]{2,1,0:T(8,128)(2,1)} %bitcast.39), calls=%async_computation.1 | async-start | bytes 4194304 | tf_op jit(solution)/shard_map/all_to_all | solution.py:446
  63.7 11.7 %collective-permute-start.1 = (bf16[96,2048]{1,0:T(8,128)(2,1)S(1)}, bf16[96,2048]{1,0:T(8,128)(2,1)S(1)}, u32[]{:S(2)}, u32[]{:S(2)}) collective-permute-start(bf16[96,2048]{1,0:T(8,128)(2,1)S(1)} %get-tuple-element.27), channel_id=1, source_target_pairs={{0,32},{8,40},{16,48},{24,56},{32,64},{40,72},{48,80},{56,88},{64,... | collective-permute-start | bytes 1179656 | tf_op jit(solution)/shard_map/ppermute | solution.py:277
  64.7 10.8 %collective-permute-start = (bf16[96,2048]{1,0:T(8,128)(2,1)S(1)}, bf16[96,2048]{1,0:T(8,128)(2,1)S(1)}, u32[]{:S(2)}, u32[]{:S(2)}) collective-permute-start(bf16[96,2048]{1,0:T(8,128)(2,1)S(1)} %copy-done.6), channel_id=1, source_target_pairs={{0,224},{8,232},{16,240},{24,248},{32,0},{40,8},{48,16},{56,24},{6... | collective-permute-start | bytes 1179656 | tf_op jit(solution)/shard_map/ppermute | solution.py:276
  79.3 19.5 %collective-permute-start.5 = (bf16[192,2048]{1,0:T(8,128)(2,1)}, bf16[192,2048]{1,0:T(8,128)(2,1)S(1)}, u32[]{:S(2)}, u32[]{:S(2)}) collective-permute-start(bf16[192,2048]{1,0:T(8,128)(2,1)} %get-tuple-element.31), channel_id=1, source_target_pairs={{0,32},{8,40},{16,48},{24,56},{32,64},{40,72},{48,80},{56,88},{64,... | collective-permute-start | bytes 2359304 | tf_op jit(solution)/shard_map/ppermute | solution.py:277
  79.9 18.9 %collective-permute-start.4 = (bf16[192,2048]{1,0:T(8,128)(2,1)S(1)}, bf16[192,2048]{1,0:T(8,128)(2,1)}, u32[]{:S(2)}, u32[]{:S(2)}) collective-permute-start(bf16[192,2048]{1,0:T(8,128)(2,1)S(1)} %get-tuple-element.28.after_ref), channel_id=1, source_target_pairs={{0,224},{8,232},{16,240},{24,248},{32,0},{40,8},{48,16},{56,24},{6... | collective-permute-start | bytes 2359304 | tf_op jit(solution)/shard_map/ppermute | solution.py:276
  93.5 13.8 %collective-permute-start.3 = (bf16[96,2048]{1,0:T(8,128)(2,1)S(1)}, bf16[96,2048]{1,0:T(8,128)(2,1)S(1)}, u32[]{:S(2)}, u32[]{:S(2)}) collective-permute-start(bf16[96,2048]{1,0:T(8,128)(2,1)S(1)} %get-tuple-element.30), channel_id=1, source_target_pairs={{0,32},{8,40},{16,48},{24,56},{32,64},{40,72},{48,80},{56,88},{64,... | collective-permute-start | bytes 1179656 | tf_op jit(solution)/shard_map/ppermute | solution.py:277
  94.5 12.8 %collective-permute-start.2 = (bf16[96,2048]{1,0:T(8,128)(2,1)S(1)}, bf16[96,2048]{1,0:T(8,128)(2,1)S(1)}, u32[]{:S(2)}, u32[]{:S(2)}) collective-permute-start(bf16[96,2048]{1,0:T(8,128)(2,1)S(1)} %get-tuple-element.29.after_ref), channel_id=1, source_target_pairs={{0,224},{8,232},{16,240},{24,248},{32,0},{40,8},{48,16},{56,24},{6... | collective-permute-start | bytes 1179656 | tf_op jit(solution)/shard_map/ppermute | solution.py:276
  102.0 22.1 %collective-permute-start.9 = (bf16[192,2048]{1,0:T(8,128)(2,1)S(1)}, bf16[192,2048]{1,0:T(8,128)(2,1)S(1)}, u32[]{:S(2)}, u32[]{:S(2)}) collective-permute-start(bf16[192,2048]{1,0:T(8,128)(2,1)S(1)} %get-tuple-element.35), channel_id=1, source_target_pairs={{0,32},{8,40},{16,48},{24,56},{32,64},{40,72},{48,80},{56,88},{64,... | collective-permute-start | bytes 2359304 | tf_op jit(solution)/shard_map/ppermute | solution.py:277
  102.3 21.8 %collective-permute-start.8 = (bf16[192,2048]{1,0:T(8,128)(2,1)S(1)}, bf16[192,2048]{1,0:T(8,128)(2,1)S(1)}, u32[]{:S(2)}, u32[]{:S(2)}) collective-permute-start(bf16[192,2048]{1,0:T(8,128)(2,1)S(1)} %get-tuple-element.32.after_ref), channel_id=1, source_target_pairs={{0,224},{8,232},{16,240},{24,248},{32,0},{40,8},{48,16},{56,24},{6... | collective-permute-start | bytes 2359304 | tf_op jit(solution)/shard_map/ppermute | solution.py:276
  110.3 30.6 %collective-permute-start.7 = (bf16[192,2048]{1,0:T(8,128)(2,1)S(1)}, bf16[192,2048]{1,0:T(8,128)(2,1)S(1)}, u32[]{:S(2)}, u32[]{:S(2)}) collective-permute-start(bf16[192,2048]{1,0:T(8,128)(2,1)S(1)} %get-tuple-element.34), channel_id=1, source_target_pairs={{0,32},{8,40},{16,48},{24,56},{32,64},{40,72},{48,80},{56,88},{64,... | collective-permute-start | bytes 2359304 | tf_op jit(solution)/shard_map/ppermute | solution.py:277
  110.6 30.3 %collective-permute-start.6 = (bf16[192,2048]{1,0:T(8,128)(2,1)S(1)}, bf16[192,2048]{1,0:T(8,128)(2,1)S(1)}, u32[]{:S(2)}, u32[]{:S(2)}) collective-permute-start(bf16[192,2048]{1,0:T(8,128)(2,1)S(1)} %get-tuple-element.33.after_ref), channel_id=1, source_target_pairs={{0,224},{8,232},{16,240},{24,248},{32,0},{40,8},{48,16},{56,24},{6... | collective-permute-start | bytes 2359304 | tf_op jit(solution)/shard_map/ppermute | solution.py:276
  127.2 30.6 %collective-permute-start.13 = (bf16[192,2048]{1,0:T(8,128)(2,1)S(1)}, bf16[192,2048]{1,0:T(8,128)(2,1)S(1)}, u32[]{:S(2)}, u32[]{:S(2)}) collective-permute-start(bf16[192,2048]{1,0:T(8,128)(2,1)S(1)} %get-tuple-element.39), channel_id=1, source_target_pairs={{0,32},{8,40},{16,48},{24,56},{32,64},{40,72},{48,80},{56,88},{64,... | collective-permute-start | bytes 2359304 | tf_op jit(solution)/shard_map/ppermute | solution.py:277
  127.3 30.5 %collective-permute-start.12 = (bf16[192,2048]{1,0:T(8,128)(2,1)S(1)}, bf16[192,2048]{1,0:T(8,128)(2,1)S(1)}, u32[]{:S(2)}, u32[]{:S(2)}) collective-permute-start(bf16[192,2048]{1,0:T(8,128)(2,1)S(1)} %get-tuple-element.36.after_ref), channel_id=1, source_target_pairs={{0,224},{8,232},{16,240},{24,248},{32,0},{40,8},{48,16},{56,24},{6... | collective-permute-start | bytes 2359304 | tf_op jit(solution)/shard_map/ppermute | solution.py:276
  144.0 30.6 %collective-permute-start.11 = (bf16[192,2048]{1,0:T(8,128)(2,1)S(1)}, bf16[192,2048]{1,0:T(8,128)(2,1)S(1)}, u32[]{:S(2)}, u32[]{:S(2)}) collective-permute-start(bf16[192,2048]{1,0:T(8,128)(2,1)S(1)} %get-tuple-element.38), channel_id=1, source_target_pairs={{0,32},{8,40},{16,48},{24,56},{32,64},{40,72},{48,80},{56,88},{64,... | collective-permute-start | bytes 2359304 | tf_op jit(solution)/shard_map/ppermute | solution.py:277
  144.1 30.5 %collective-permute-start.10 = (bf16[192,2048]{1,0:T(8,128)(2,1)S(1)}, bf16[192,2048]{1,0:T(8,128)(2,1)S(1)}, u32[]{:S(2)}, u32[]{:S(2)}) collective-permute-start(bf16[192,2048]{1,0:T(8,128)(2,1)S(1)} %get-tuple-element.37.after_ref), channel_id=1, source_target_pairs={{0,224},{8,232},{16,240},{24,248},{32,0},{40,8},{48,16},{56,24},{6... | collective-permute-start | bytes 2359304 | tf_op jit(solution)/shard_map/ppermute | solution.py:276
  178.4 25.5 %collective-permute-start.15 = (bf16[192,2048]{1,0:T(8,128)(2,1)}, bf16[192,2048]{1,0:T(8,128)(2,1)}, u32[]{:S(2)}, u32[]{:S(2)}) collective-permute-start(bf16[192,2048]{1,0:T(8,128)(2,1)} %get-tuple-element.44), channel_id=1, source_target_pairs={{0,32},{8,40},{16,48},{24,56},{32,64},{40,72},{48,80},{56,88},{64,... | collective-permute-start | bytes 2359304 | tf_op jit(solution)/shard_map/ppermute | solution.py:277
  178.4 25.5 %collective-permute-start.14 = (bf16[192,2048]{1,0:T(8,128)(2,1)S(1)}, bf16[192,2048]{1,0:T(8,128)(2,1)}, u32[]{:S(2)}, u32[]{:S(2)}) collective-permute-start(bf16[192,2048]{1,0:T(8,128)(2,1)S(1)} %get-tuple-element.40.refs_5_), channel_id=1, source_target_pairs={{0,224},{8,232},{16,240},{24,248},{32,0},{40,8},{48,16},{56,24},{6... | collective-permute-start | bytes 2359304 | tf_op jit(solution)/shard_map/ppermute | solution.py:276
  181.1 26.6 %all-to-all-start.2 = ((bf16[4,48,2048]{2,1,0:T(8,128)(2,1)}), bf16[4,48,2048]{2,1,0:T(8,128)(2,1)S(1)}, u32[]{:S(2)}, u32[]{:S(2)}) async-start(bf16[4,48,2048]{2,1,0:T(8,128)(2,1)} %bitcast.15), calls=%async_computation.2 | async-start | bytes 1572864 | tf_op jit(solution)/shard_map/all_to_all | solution.py:286
  203.9 23.2 %copy-start.13 = (s32[512,8]{0,1:T(8,128)S(1)}, s32[512,8]{0,1:T(8,128)}, u32[]{:S(2)}) copy-start(s32[512,8]{0,1:T(8,128)} %param.6) | copy-start | bytes 49156
  207.7 20.6 %all-to-all-start.3 = ((bf16[4,48,2048]{2,1,0:T(8,128)(2,1)}), bf16[4,48,2048]{2,1,0:T(8,128)(2,1)S(1)}, u32[]{:S(2)}, u32[]{:S(2)}) async-start(bf16[4,48,2048]{2,1,0:T(8,128)(2,1)} %bitcast.16), calls=%async_computation.3 | async-start | bytes 1572864 | tf_op jit(solution)/shard_map/all_to_all | solution.py:286
  (15 other events, 85.2 us)
Sparse Core Ops, SparseCore 0:
  9.8 48.5 all-gather.4
  60.2 120.0 all-gather.6
